TPU v7x, 32 devices: a whole 2x2x4 slice. The times are simulated.
32 devices in a mesh: dp: 4 (over y, x), mp: 8 (over z, core).
Axes of the slice: x: 2, y: 2, z: 4, core: 2. Of those that a mesh axis runs over, the one named last changes fastest.
Arguments:
- hidden_states: bfloat16 [2048, 4096], P('dp', 'mp'), may hold values from -6 to 6
- gate_online: bfloat16 [4096, 14336], P('dp', 'mp'), may hold values from -0.09375 to 0.09375
- up_online: bfloat16 [4096, 14336], P('dp', 'mp'), may hold values from -0.09375 to 0.09375
- down_online: bfloat16 [14336, 4096], P('mp', 'dp'), may hold values from -0.046875 to 0.046875
- gate_previous: bfloat16 [4096, 14336], P(None, 'mp'), may hold values from -0.09375 to 0.09375
- up_previous: bfloat16 [4096, 14336], P(None, 'mp'), may hold values from -0.09375 to 0.09375
- down_previous: bfloat16 [14336, 4096], P('mp'), may hold values from -0.046875 to 0.046875
Outputs:
- online_output: bfloat16 [2048, 4096], P('dp', 'mp')
- target_output: bfloat16 [2048, 4096], P('dp', 'mp')
All inputs are finite; a program needn't handle non-finite values.
Results may differ from a plain program's by a relative error of at most 0.0072.
Values may be sent and summed in bfloat16 or wider, within the bound.
No kernel may reach another device: no remote copies, remote signals or barrier semaphores. Data moves between devices by JAX's collectives and lax.ppermute only.
A program may use at most 192 MiB of HBM per device.

v0:
```python
import jax
import jax.numpy as jnp
from jax import lax
from jax.sharding import PartitionSpec as P

POLYAK = 0.25


def blend(online, previous):
    return (
        POLYAK * online.astype(jnp.float32) + (1.0 - POLYAK) * previous.astype(jnp.float32)
    ).astype(jnp.bfloat16)


def add_pair(features_all, piece, previous):
    target_piece = blend(piece, previous)
    online_sum = jnp.dot(features_all, piece, preferred_element_type=jnp.float32)
    target_sum = jnp.dot(features_all, target_piece, preferred_element_type=jnp.float32)
    return (online_sum, target_sum)


def local(
    hidden_states, gate_online, up_online, down_online, gate_previous, up_previous, down_previous
):
    features_all = lax.all_gather(hidden_states, "mp", axis=1, tiled=True)
    gate_o, gate_t = add_pair(
        features_all, lax.all_gather(gate_online, "dp", axis=0, tiled=True), gate_previous
    )
    up_o, up_t = add_pair(
        features_all, lax.all_gather(up_online, "dp", axis=0, tiled=True), up_previous
    )
    inner_o = (jax.nn.silu(gate_o) * up_o).astype(jnp.bfloat16)
    inner_t = (jax.nn.silu(gate_t) * up_t).astype(jnp.bfloat16)
    piece = lax.all_gather(down_online, "dp", axis=1, tiled=True)
    target_piece = blend(piece, down_previous)
    online_part = jnp.dot(inner_o, piece, preferred_element_type=jnp.float32)
    target_part = jnp.dot(inner_t, target_piece, preferred_element_type=jnp.float32)
    terms = jnp.stack([online_part, target_part], axis=0)
    summed = lax.psum_scatter(terms, "mp", scatter_dimension=2, tiled=True)
    result = summed.astype(jnp.bfloat16)
    return (result[0], result[1])


def solution(mesh):
    in_specs = (
        P("dp", "mp"),
        P("dp", "mp"),
        P("dp", "mp"),
        P("mp", "dp"),
        P(None, "mp"),
        P(None, "mp"),
        P("mp", None),
    )
    out_specs = (P("dp", "mp"), P("dp", "mp"))
    return jax.shard_map(local, mesh=mesh, in_specs=in_specs, out_specs=out_specs, check_vma=False)
```

profile of v0, /device:TPU:0, one launch (start us, length us, event | category | flops | bytes accessed | tf_op | source)
XLA Modules:
  0.0 735.3 jit_solution(5018734228130765763)
XLA Ops:
  7.2 0.0 all-gather.5.cloned.1.call-start
  7.2 0.7 all-gather.5.cloned.1.call-update
  7.9 0.0 all-gather.7.cloned.1.call-start
  7.9 0.7 all-gather.7.cloned.1.call-update
  8.6 0.0 all-gather.9.cloned.1.call-start
  8.7 0.7 all-gather.9.cloned.1.call-update
  9.4 0.0 all-gather.11.cloned.1.call-start
  9.4 0.5 all-gather.11.cloned.1.call-update
  10.0 0.0 reduce-scatter.2.cloned.1.call-start
  10.0 49.5 %all-gather.5.cloned.1.call-done = bf16[512,4096]{1,0:T(8,128)(2,1)} async-done(((bf16[512,512]{1,0:T(8,128)(2,1)}), bf16[512,4096]{1,0:T(8,128)(2,1)}) %all-gather.5.cloned.1.call-update) | async-done | bytes 4194320 | tf_op jit(solution)/shard_map/all_gather | solution.py:25
  59.5 140.6 %all-gather.7.cloned.1.call-done = bf16[4096,1792]{1,0:T(8,128)(2,1)} async-done(((bf16[1024,1792]{1,0:T(8,128)(2,1)}), bf16[4096,1792]{1,0:T(8,128)(2,1)}) %all-gather.7.cloned.1.call-update) | async-done | bytes 14680080 | tf_op jit(solution)/shard_map/all_gather | solution.py:27
  200.0 0.0 copy-start
  200.0 16.5 %fusion.24 = f32[512,1792]{1,0:T(8,128)} fusion(bf16[512,4096]{1,0:T(8,128)(2,1)} %all-gather.5.cloned.1.call-done, bf16[4096,1792]{1,0:T(8,128)(2,1)} %all-gather.7.cloned.1.call-done), kind=kOutput, calls=%fused_computation.33 | convolution fusion | flops 7516192768 | bytes 22544384 | tf_op jit(solution)/shard_map/dot_general | solution.py:17
  216.6 0.0 copy-done
  216.6 14.9 %fusion = f32[1792,512]{0,1:T(8,128)} fusion(bf16[512,4096]{1,0:T(8,128)(2,1)S(1)} %copy-done, bf16[4096,1792]{1,0:T(8,128)(2,1)} %param.11, bf16[4096,1792]{1,0:T(8,128)(2,1)} %all-gather.7.cloned.1.call-done), kind=kOutput, calls=%fused_computation.4 | convolution fusion | flops 7560232960 | bytes 37224448 | tf_op jit(solution)/shard_map/dot_general | solution.py:18
  231.5 110.4 %all-gather.9.cloned.1.call-done = bf16[4096,1792]{1,0:T(8,128)(2,1)} async-done(((bf16[1024,1792]{1,0:T(8,128)(2,1)}), bf16[4096,1792]{1,0:T(8,128)(2,1)}) %all-gather.9.cloned.1.call-update) | async-done | bytes 14680080 | tf_op jit(solution)/shard_map/all_gather | solution.py:30
  341.9 141.7 %all-gather.11.cloned.1.call-done = bf16[1792,4096]{1,0:T(8,128)(2,1)} async-done(((bf16[1792,1024]{1,0:T(8,128)(2,1)}), bf16[1792,4096]{1,0:T(8,128)(2,1)}) %all-gather.11.cloned.1.call-update) | async-done | bytes 14680080 | tf_op jit(solution)/shard_map/all_gather | solution.py:34
  483.6 31.3 %convolution_bitcast_fusion = f32[1,512,4096]{2,1,0:T(8,128)} fusion(bf16[1792,4096]{1,0:T(8,128)(2,1)} %all-gather.11.cloned.1.call-done, f32[512,1792]{1,0:T(8,128)} %fusion.24, bf16[512,4096]{1,0:T(8,128)(2,1)} %all-gather.5.cloned.1.call-done, bf16[4096,1792]{1,0:T(8,128)(2,1)} %all-gather.9.cloned.1.call-done), kind=kOutput, calls=%fused_computation.14 | convolution fusion | flops 15037890560 | bytes 45613056 | tf_op jit(solution)/shard_map/dot_general | solution.py:36
  514.9 31.1 %fusion.9 = f32[1,512,4096]{2,1,0:T(8,128)} fusion(bf16[1792,4096]{1,0:T(8,128)(2,1)} %param.13, bf16[1792,4096]{1,0:T(8,128)(2,1)} %all-gather.11.cloned.1.call-done, f32[1792,512]{0,1:T(8,128)} %fusion, bf16[512,4096]{1,0:T(8,128)(2,1)} %all-gather.5.cloned.1.call-done, bf16[4096,1792]{1,0:T(8,128)(2,1)} %param.12, ...), kind=kOutput, calls=%fused_computation.13 | convolution fusion | flops 15125970944 | bytes 74973184 | tf_op jit(solution)/shard_map/dot_general | solution.py:37
  546.0 11.6 %pad_maximum_fusion = f32[2,512,4096]{2,1,0:T(8,128)} fusion(f32[1,512,4096]{2,1,0:T(8,128)} %fusion.9, f32[1,512,4096]{2,1,0:T(8,128)} %convolution_bitcast_fusion), kind=kLoop, calls=%fused_computation.3 | loop fusion | flops 4194304 | bytes 33554432 | tf_op jit(solution)/shard_map/stack | solution.py:38
  557.6 0.0 reduce-scatter.2.cloned.1.call-update
  557.6 168.4 %reduce-scatter.2.cloned.1.call-done = f32[2,512,512]{2,1,0:T(8,128)} async-done(((f32[2,512,4096]{2,1,0:T(8,128)}), f32[2,512,512]{2,1,0:T(8,128)}) %reduce-scatter.2.cloned.1.call-update) | async-done | bytes 2097168 | tf_op jit(solution)/shard_map/reduce_scatter | solution.py:39
  726.0 1.7 convert_element_type.47
  727.7 1.0 slice_bitcast_fusion
Async XLA Ops:
  7.2 52.3 %all-gather.5.cloned.1.call-start = ((), (), s32[]{:S(2)}) async-start(), calls=%async_computation.1 | async-start | bytes 4718592 | tf_op jit(solution)/shard_map/all_gather | solution.py:25
  7.9 192.1 %all-gather.7.cloned.1.call-start = ((), (), s32[]{:S(2)}) async-start(), calls=%async_computation.2 | async-start | bytes 18350080 | tf_op jit(solution)/shard_map/all_gather | solution.py:27
  8.6 333.2 %all-gather.9.cloned.1.call-start = ((), (), s32[]{:S(2)}) async-start(), calls=%async_computation.3 | async-start | bytes 18350080 | tf_op jit(solution)/shard_map/all_gather | solution.py:30
  9.4 474.2 %all-gather.11.cloned.1.call-start = ((), (), s32[]{:S(2)}) async-start(), calls=%async_computation.4 | async-start | bytes 18350080 | tf_op jit(solution)/shard_map/all_gather | solution.py:34
  10.0 716.0 %reduce-scatter.2.cloned.1.call-start = ((), (), s32[]{:S(2)}) async-start(), calls=%async_computation.5 | async-start | bytes 18874368 | tf_op jit(solution)/shard_map/reduce_scatter | solution.py:39
  200.0 16.5 %copy-start = (bf16[512,4096]{1,0:T(8,128)(2,1)S(1)}, bf16[512,4096]{1,0:T(8,128)(2,1)}, u32[]{:S(2)}) copy-start(bf16[512,4096]{1,0:T(8,128)(2,1)} %all-gather.5.cloned.1.call-done) | copy-start | bytes 12582916
Sparse Core Ops, SparseCore 0:
  9.6 49.8 all-gather.4
  61.3 138.6 all-gather.6
  201.9 139.9 all-gather.8
  343.6 139.9 all-gather.10
  557.7 168.2 reduce-scatter.1
where the time goes:
time: 735 us
  waiting for transfers between devices  613 us (83%)
  matrix products  93.8 us (13%)
  between operations  13.8 us (2%)
  other arithmetic  13.3 us (2%)
    reduce_scatter x1, waiting for transfers between devices, local(): summed = lax.psum_scatter(terms, 'mp', scatter_dimension=2, tiled=True)  168 us
    all_gather x1, waiting for transfers between devices, local(): piece = lax.all_gather(down_online, 'dp', axis=1, tiled=True)  142 us
    all_gather x1, waiting for transfers between devices, local(): lax.all_gather(gate_online, 'dp', axis=0, tiled=True)  141 us
    all_gather x1, waiting for transfers between devices, local(): lax.all_gather(up_online, 'dp', axis=0, tiled=True)  110 us
    all_gather x1, waiting for transfers between devices, local(): features_all = lax.all_gather(hidden_states, 'mp', axis=1, tiled=True)  49.5 us
    dot_general x1, matrix products, local(): online_part = jnp.dot(inner_o, piece, preferred_element_type=jnp.float32)  31.3 us
    dot_general x1, matrix products, local(): jnp.dot(inner_t, target_piece, preferred_element_type=jnp.float32)  31.1 us
    dot_general x1, matrix products, add_pair(): jnp.dot(features_all, piece, preferred_element_type=jnp.float32)  16.5 us
  transfers between devices with their start and end apart: 5, of which 5 were waited for; matrix products, arithmetic and copies ran while one was open for 4% of the time, Pallas kernels for 0%

commit v1 on v0

v1 whole, which is shorter than its diff:
```python
import functools

import jax
import jax.numpy as jnp
from jax import lax
from jax.experimental import pallas as pl
from jax.experimental.pallas import tpu as pltpu
from jax.sharding import PartitionSpec as P

POLYAK = 0.25
TILE = 1024
VMEM_BYTES = 56 * 1024 * 1024
CHEAP = pl.CostEstimate(flops=1, bytes_accessed=1, transcendentals=0)


def blend(online, previous):
    return (
        POLYAK * online.astype(jnp.float32) + (1.0 - POLYAK) * previous.astype(jnp.float32)
    ).astype(jnp.bfloat16)


def dot(a, b):
    return jnp.dot(a, b, preferred_element_type=jnp.float32)


def silu(v):
    return v / (1.0 + jnp.exp(-v))


def hidden_kernel(n, n_start, n_gates, n_after, order, *refs):
    refs = list(refs)

    def take(count):
        out = refs[:count]
        del refs[:count]
        return out

    (features,) = take(1)
    online, (previous,) = take(n), take(1)
    more = take(n_start + n_gates)
    take(n_after)
    outs = take(2)
    f_buf, on_buf, old_buf = take(3)
    more_buf = take(len(more))
    acc = take(2)
    target, sems = take(2)
    rows, units = on_buf.shape[1:]
    tokens = f_buf.shape[1]
    copies = []
    for k in range(n):
        at = pl.ds(pl.multiple_of(order[k] * rows, rows), rows)
        old = previous.at[at]
        if previous.shape[1] != units:
            old = old.at[:, pl.ds(pl.multiple_of(order[n], 128), units)]
        group = [
            pltpu.make_async_copy(online[k], on_buf.at[k], sems.at[3 * k]),
            pltpu.make_async_copy(old, old_buf.at[k], sems.at[3 * k + 1]),
            pltpu.make_async_copy(features.at[:, at], f_buf.at[k], sems.at[3 * k + 2]),
        ]
        for copy in group:
            copy.start()
        copies.append(group)
    last = [
        pltpu.make_async_copy(src, dst, sems.at[3 * n + m])
        for m, (src, dst) in enumerate(zip(more, more_buf))
    ]
    for copy in last:
        copy.start()
    tile = min(TILE, tokens)
    starts = more_buf[:n_start]
    gates = more_buf[n_start:]
    for k in range(n):
        for copy in copies[k]:
            copy.wait()
        target[...] = blend(on_buf[k], old_buf[k])
        if k == n - 1:
            for copy in last:
                copy.wait()

        @pl.loop(0, tokens // tile)
        def _(t):
            here = pl.ds(pl.multiple_of(t * tile, tile), tile)
            f = f_buf[k, here, :]
            for m, w in enumerate((on_buf.at[k], target)):
                s = dot(f, w[...])
                if k > 0:
                    s = s + acc[m][here, :]
                if k == n - 1:
                    if starts:
                        s = s + starts[m][here, :]
                    if gates:
                        s = silu(gates[m][here, :]) * s
                    outs[m][here, :] = s.astype(outs[m].dtype)
                else:
                    acc[m][here, :] = s


def hidden_pair(features, order, pieces, previous, start=(), gates=(), after=()):
    n = len(pieces)
    rows, units = pieces[0].shape
    tokens = features.shape[0]
    kind = jnp.bfloat16 if gates else jnp.float32
    shape = jax.ShapeDtypeStruct((tokens, units), kind)
    anywhere = pl.BlockSpec(memory_space=pl.ANY)
    args = [features, *pieces, previous, *start, *gates, *after]
    wide = pltpu.VMEM((tokens, units), jnp.float32)
    n_more = len(start) + len(gates)
    block = pltpu.VMEM((n, rows, units), jnp.bfloat16)
    return pl.pallas_call(
        functools.partial(hidden_kernel, n, len(start), len(gates), len(after)),
        in_specs=[pl.BlockSpec(memory_space=pltpu.SMEM)] + [anywhere] * len(args),
        out_specs=[pl.BlockSpec(memory_space=pltpu.VMEM)] * 2,
        scratch_shapes=[pltpu.VMEM((n, tokens, rows), jnp.bfloat16), block, block]
        + [wide] * (n_more + 2)
        + [pltpu.VMEM((rows, units), jnp.bfloat16), pltpu.SemaphoreType.DMA((3 * n + n_more,))],
        out_shape=[shape, shape],
        compiler_params=pltpu.CompilerParams(vmem_limit_bytes=VMEM_BYTES),
        cost_estimate=CHEAP,
    )(jnp.stack(order).astype(jnp.int32), *args)


def down_kernel(n, ny, n_after, at, *refs):
    inner = refs[0:2], refs[2:4]
    online, previous = refs[4 : 4 + n], (refs[4 + n : 4 + 2 * n], refs[4 + 2 * n : 4 + 3 * n])
    *gives, keep, w_o, w_t = refs[4 + 3 * n + n_after :]
    tokens, units = inner[0][0].shape
    step = online[0].shape[1]
    for k in range(n):
        here = slice(k * step, (k + 1) * step)
        w_o[:, here] = online[k][...]
        for e in range(2):
            rows = slice(e * units, (e + 1) * units)
            w_t[rows, here] = blend(online[k][rows, :], previous[e][k][...])
    for m, ((own, other), w) in enumerate(zip(inner, (w_o, w_t))):
        s = dot(own[...], w[:units, :]) + dot(other[...], w[units:, :])
        for r, out in enumerate((keep, *gives)):
            rows = slice(r * tokens // ny, (r + 1) * tokens // ny)
            for k in range(n):
                out[at[k], m] = s[rows, k * step : (k + 1) * step].astype(out.dtype)


def down_pair(inner, pieces, blocks, piece_at, old, own_at, other_at, y, step, ny, after):
    n = len(pieces)
    tokens, units = inner[0].shape
    at = [*blocks, *piece_at, *own_at, *other_at, y]
    shape = (n, 2, tokens // ny, step)

    def columns(rows, k, row=lambda w: 0):
        return pl.BlockSpec((rows, step), lambda g, w: (row(w), w[k]))

    return pl.pallas_call(
        functools.partial(down_kernel, n, ny, len(after)),
        grid_spec=pltpu.PrefetchScalarGridSpec(
            num_scalar_prefetch=1,
            grid=(1,),
            in_specs=[pl.BlockSpec((tokens, units), lambda g, w: (0, 0))] * 4
            + [columns(2 * units, n + k) for k in range(n)]
            + [columns(units, 2 * n + k, lambda w: w[4 * n]) for k in range(n)]
            + [columns(units, 3 * n + k) for k in range(n)]
            + [pl.BlockSpec(memory_space=pl.ANY)] * len(after),
            out_specs=[pl.BlockSpec(shape, lambda g, w: (0, 0, 0, 0))] * ny,
            scratch_shapes=[pltpu.VMEM((2 * units, n * step), jnp.bfloat16)] * 2,
        ),
        out_shape=[jax.ShapeDtypeStruct(shape, jnp.bfloat16)] * (ny - 1)
        + [jax.ShapeDtypeStruct(shape, jnp.float32)],
        compiler_params=pltpu.CompilerParams(
            dimension_semantics=("arbitrary",), vmem_limit_bytes=VMEM_BYTES
        ),
        cost_estimate=CHEAP,
    )(
        jnp.stack(at).astype(jnp.int32),
        *inner,
        *pieces,
        *[old[0]] * n,
        *[old[1]] * n,
        *after,
    )


def cut_kernel(at, src, out):
    del at
    out[...] = src[...]


def cut_old(previous, y, h, rows, width):
    n = previous.shape[1] // (2 * width)
    return pl.pallas_call(
        cut_kernel,
        grid_spec=pltpu.PrefetchScalarGridSpec(
            num_scalar_prefetch=1,
            grid=(n,),
            in_specs=[pl.BlockSpec((rows, width), lambda b, at: (at[0], 2 * b + at[1]))],
            out_specs=pl.BlockSpec((rows, width), lambda b, at: (0, b)),
        ),
        out_shape=jax.ShapeDtypeStruct((rows, n * width), previous.dtype),
        cost_estimate=CHEAP,
    )(jnp.stack([y, h]).astype(jnp.int32), previous)


def add_kernel(n_after, keep, *refs):
    *got, out = refs[: len(refs) - 1 - n_after] + refs[-1:]
    total = keep[...]
    for v in got:
        total = total + v[...].astype(jnp.float32)
    out[...] = total.astype(out.dtype)


def add_all(keep, got, after):
    block = pl.BlockSpec((1, *keep.shape[1:]), lambda q: (q, 0, 0, 0))
    return pl.pallas_call(
        functools.partial(add_kernel, len(after)),
        grid=(keep.shape[0],),
        in_specs=[block] * (1 + len(got)) + [pl.BlockSpec(memory_space=pl.ANY)] * len(after),
        out_specs=block,
        out_shape=jax.ShapeDtypeStruct(keep.shape, jnp.bfloat16),
        compiler_params=pltpu.CompilerParams(vmem_limit_bytes=VMEM_BYTES),
        cost_estimate=CHEAP,
    )(keep, *got, *after)


def make_local(n_dp, n_mp):
    ny, nz = n_dp // 2, n_mp // 2
    assert nz == n_dp and n_dp % 2 == 0
    along_x = [(i, i ^ 1) for i in range(n_dp)]
    along_core = [(j, j ^ 1) for j in range(n_mp)]

    def along_y(r):
        return [(y * 2 + x, ((y + r) % ny) * 2 + x) for y in range(ny) for x in range(2)]

    same_core = [[2 * z + c for z in range(nz)] for c in range(2)]

    def local(hidden, gate_on, up_on, down_on, gate_prev, up_prev, down_prev):
        i, j = lax.axis_index("dp"), lax.axis_index("mp")
        y, x = i // 2, i % 2
        c = j % 2
        units = gate_on.shape[1]
        own_units = units // ny
        tokens = hidden.shape[0]

        def before(r):
            return lax.rem(y + (ny - r), ny)

        def swap_units(w, axis):
            out = []
            for r in range(ny):
                start = lax.rem(y + r, ny) * own_units
                piece = lax.dynamic_slice_in_dim(w, start, own_units, axis)
                out.append(piece if r == 0 else lax.ppermute(piece, "dp", along_y(r)))
            return out

        def from_x(pieces):
            return [lax.ppermute(p, "dp", along_x) for p in pieces]

        gate_near = swap_units(gate_on, 1)
        up_near = swap_units(up_on, 1)
        cols = down_on.shape[1]
        half = cols // 2
        down_mine = lax.dynamic_slice_in_dim(down_on, c * half, half, 1)
        down_give = lax.dynamic_slice_in_dim(down_on, (1 - c) * half, half, 1)
        down_pairs = [down_mine, lax.ppermute(down_give, "mp", along_core)]
        down_near = []
        for r in range(ny):
            start = lax.rem(y + r, ny) * own_units
            piece = jnp.concatenate(
                [lax.dynamic_slice_in_dim(w, start, own_units, 0) for w in down_pairs], 0
            )
            down_near.append(piece if r == 0 else lax.ppermute(piece, "dp", along_y(r)))
        gate_far, up_far = from_x(gate_near), from_x(up_near)
        mine = [hidden] + [lax.ppermute(hidden, "dp", along_y(r)) for r in range(1, ny)]
        mine, *_ = lax.optimization_barrier((mine, gate_near[0], up_near[0]))
        features = lax.all_gather(jnp.concatenate(mine, 0), "mp", axis=1, tiled=True)

        near = [before(r) * 2 + x for r in range(ny)]
        far = [before(r) * 2 + (1 - x) for r in range(ny)]
        first = y * own_units
        gate_old, up_old = gate_prev, up_prev
        if own_units % 128:
            gate_old = lax.dynamic_slice_in_dim(gate_prev, first, own_units, 1)
            up_old = lax.dynamic_slice_in_dim(up_prev, first, own_units, 1)
        old_other = lax.ppermute(cut_old(down_prev, y, 1 - c, own_units, half), "mp", along_core)

        gate_part = hidden_pair(features, [*near, first], gate_near, gate_old)
        up_part = hidden_pair(features, [*near, first], up_near, up_old)
        step = 128
        jobs = half // step
        down_send = [
            jnp.concatenate([p[:, s * step : (s + 1) * step] for p in down_near], 1)
            for s in range(jobs)
        ]
        down_far = from_x(down_send)

        gates = hidden_pair(features, [*far, first], gate_far, gate_old, start=gate_part)
        inner_o, inner_t = hidden_pair(
            features,
            [*far, first],
            up_far,
            up_old,
            start=up_part,
            gates=gates,
            after=down_send,
        )

        (inner_o, inner_t), down_far[0] = lax.optimization_barrier(
            ((inner_o, inner_t), down_far[0])
        )
        inner = []
        for v in (inner_o, inner_t):
            inner += [v, lax.ppermute(v, "mp", along_core)]

        def products(s, after):
            *gives, keep = down_pair(
                inner,
                down_near + [down_far[s]] * ny,
                near + far,
                [s + 0 * c] * ny + [k + 0 * c for k in range(ny)],
                (down_prev, old_other),
                [(b * 2 + c) * jobs + s for b in near + far],
                [b * jobs + s for b in near + far],
                y,
                step,
                ny,
                after,
            )
            return keep, gives, [
                lax.ppermute(v, "dp", along_y(ny - 1 - r)) for r, v in enumerate(gives)
            ]

        def over_z(keep, from_y, earlier):
            total = add_all(keep, from_y, earlier)
            summed = lax.psum_scatter(
                total, "mp", scatter_dimension=0, axis_index_groups=same_core, tiled=True
            )
            return total, summed[0]

        results = []
        total, last, waiting = [], [], None
        for s in range(jobs + 1):
            if s < jobs:
                keep, gives, from_y = products(s, last + total)
                last = gives[:1]
            if waiting is not None:
                ahead = last + results[-1:]
                if s + 1 < jobs:
                    ahead.append(down_far[s + 1])
                total, summed = over_z(*waiting, ahead)
                total = [total]
                results.append(summed)
            waiting = keep, from_y
        result = jnp.concatenate(results, -1)
        return result[0], result[1]

    return local


def solution(mesh):
    in_specs = (
        P("dp", "mp"),
        P("dp", "mp"),
        P("dp", "mp"),
        P("mp", "dp"),
        P(None, "mp"),
        P(None, "mp"),
        P("mp", None),
    )
    out_specs = (P("dp", "mp"), P("dp", "mp"))
    local = make_local(mesh.shape["dp"], mesh.shape["mp"])
    return jax.shard_map(local, mesh=mesh, in_specs=in_specs, out_specs=out_specs, check_vma=False)
```

time: 735 us -> 418 us (0.57)
  waiting for transfers between devices: 613 us -> 213 us
  Pallas kernels: 0 us -> 127 us
  matrix products: 93.8 us -> 0 us
  starting transfers between devices: 0.19 us -> 22.3 us
  local copies, waits for them, and re-layouts: 1.04 us -> 22.3 us
    all_gather x4 -> x1, waiting for transfers between devices: 442 us -> 0.01 us  [local(): lax.all_gather(jnp.concatenate(mine, 0), 'mp', axis=1, tiled=True)]
    ppermute x0 -> x20, waiting for transfers between devices: none -> 182 us  [the longest x2 65.3 us: swap_units(): out.append(piece if r == 0 else lax.ppermute(piece, 'dp', along_y(r)))]
    reduce_scatter x1 -> x4, waiting for transfers between devices: 168 us -> 31.5 us  [over_z(): lax.psum_scatter(total, 'mp', scatter_dimension=0, axis_index_groups=same...]
    pallas_call x0 -> x13, Pallas kernels: none -> 127 us  [the longest x4 59.6 us: hidden_pair(): pl.pallas_call(functools.partial(hidden_kernel, n, len(start), len(gates)...]
    dot_general x4 -> x0, matrix products: 93.8 us -> none  [the longest x1 31.3 us: local(): online_part = jnp.dot(inner_o, piece, preferred_element_type=jnp.float32)]
    ppermute x0 -> x20, starting transfers between devices: none -> 22.1 us  [the longest x8 9.57 us: from_x(): return [lax.ppermute(p, 'dp', along_x) for p in pieces]]
    dynamic_slice x0 -> x5, local copies, waits for them, and re-layouts: none -> 13.1 us  [the longest x2 6.45 us: swap_units(): piece = lax.dynamic_slice_in_dim(w, start, own_units, axis)]
    concatenate x0 -> x9, other arithmetic: none -> 13 us  [the longest x3 6.4 us: local(): jnp.concatenate([lax.dynamic_slice_in_dim(w, start, own_units, 0) for w i...]
  transfers between devices with their start and end apart: 5 -> 25, of which waited for: 5 -> 16; matrix products, arithmetic and copies ran while one was open for 4% -> 7% of each run, Pallas kernels for 0% -> 24%
where the time goes in v1:
time: 418 us; the launch traced here: 415 us
  waiting for transfers between devices  213 us (51%)
  Pallas kernels  127 us (30%)
  starting transfers between devices  22.3 us (5%)
  local copies, waits for them, and re-layouts  22.3 us (5%)
  other arithmetic  14.8 us (4%)
  between operations  14.4 us (3%)
    ppermute x2, waiting for transfers between devices, swap_units(): out.append(piece if r == 0 else lax.ppermute(piece, 'dp', along_y(r)))  65.3 us
    pallas_call x4, Pallas kernels, hidden_pair(): pl.pallas_call(functools.partial(hidden_kernel, n, len(start), len(gates)...  59.6 us
    pallas_call x4, Pallas kernels, down_pair(): pl.pallas_call(functools.partial(down_kernel, n, ny, len(after)), grid_sp...  46.6 us
    ppermute x1, waiting for transfers between devices, local(): down_near.append(piece if r == 0 else lax.ppermute(piece, 'dp', along_y(r)))  37.1 us
    ppermute x4, waiting for transfers between devices, products(): lax.ppermute(v, 'dp', along_y(ny - 1 - r))  36.9 us
    ppermute x8, waiting for transfers between devices, from_x(): return [lax.ppermute(p, 'dp', along_x) for p in pieces]  33.8 us
    reduce_scatter x4, waiting for transfers between devices, over_z(): lax.psum_scatter(total, 'mp', scatter_dimension=0, axis_index_groups=same...  31.5 us
    pallas_call x4, Pallas kernels, add_all(): pl.pallas_call(functools.partial(add_kernel, len(after)), grid=(keep.shap...  15.6 us
  transfers between devices with their start and end apart: 25, of which 16 were waited for; matrix products, arithmetic and copies ran while one was open for 7% of the time, Pallas kernels for 24%

profile of v1, /device:TPU:0, one launch (start us, length us, event | category | flops | bytes accessed | tf_op | source)
XLA Modules:
  0.0 414.7 jit_solution(9127212785330718628)
XLA Ops:
  10.2 4.3 %constant_dynamic-slice_fusion.3 = (bf16[1024,896]{1,0:T(8,128)(2,1)}, bf16[1024,896]{1,0:T(8,128)(2,1)}) fusion(bf16[1024,1792]{1,0:T(8,128)(2,1)} %param.8, s32[]{:T(128)S(6)} %select_n.43, s32[]{:T(128)S(6)} %select_n.42), kind=kLoop, calls=%fused_computation.25 | loop fusion | bytes 7340040 | tf_op jit(solution)/shard_map/dynamic_slice | solution.py:247
  16.7 5.7 %collective-permute-done = bf16[512,512]{1,0:T(8,128)(2,1)S(1)} collective-permute-done((bf16[512,512]{1,0:T(8,128)(2,1)}, bf16[512,512]{1,0:T(8,128)(2,1)S(1)}, u32[]{:S(2)}, u32[]{:S(2)}) %collective-permute-start) | collective-permute-done | bytes 524320 | tf_op jit(solution)/shard_map/ppermute | solution.py:269
  37.9 5.6 %shard_map.90 = bf16[896,2048]{1,0:T(8,128)(2,1)} custom-call(s32[2]{0:T(128)} %pad_add_fusion.at, bf16[1792,4096]{1,0:T(8,128)(2,1)} %refs_11_.7), custom_call_target="tpu_custom_call" | custom-call | flops 1 | bytes 1 | tf_op jit(solution)/shard_map/pallas_call | solution.py:187
  43.6 26.0 %collective-permute-done.5.refs_2_ = bf16[1024,896]{1,0:T(8,128)(2,1)} collective-permute-done((bf16[1024,896]{1,0:T(8,128)(2,1)}, bf16[1024,896]{1,0:T(8,128)(2,1)}, u32[]{:S(2)}, u32[]{:S(2)}) %collective-permute-start.5) | collective-permute-done | bytes 1835040 | tf_op jit(solution)/shard_map/ppermute | solution.py:248
  69.5 39.3 %collective-permute-done.2.refs_2_ = bf16[1024,896]{1,0:T(8,128)(2,1)} collective-permute-done((bf16[1024,896]{1,0:T(8,128)(2,1)}, bf16[1024,896]{1,0:T(8,128)(2,1)}, u32[]{:S(2)}, u32[]{:S(2)}) %collective-permute-start.2) | collective-permute-done | bytes 1835040 | tf_op jit(solution)/shard_map/ppermute | solution.py:248
  110.6 37.1 %collective-permute-done.8.refs_5_ = bf16[1792,512]{1,0:T(8,128)(2,1)S(1)} collective-permute-done((bf16[1792,512]{1,0:T(8,128)(2,1)}, bf16[1792,512]{1,0:T(8,128)(2,1)S(1)}, u32[]{:S(2)}, u32[]{:S(2)}) %collective-permute-start.8) | collective-permute-done | bytes 1835040 | tf_op jit(solution)/shard_map/ppermute | solution.py:267
  159.6 14.4 %shard_map.87 = (f32[1024,896]{1,0:T(8,128)}, f32[1024,896]{1,0:T(8,128)}) custom-call(s32[3]{0:T(128)} %add_add_fusion.1.order, bf16[1024,4096]{1,0:T(8,128)(2,1)} %all-gather.2.cloned.1.call-done.refs_0_, bf16[1024,896]{1,0:T(8,128)(2,1)} %get-tuple-element.47.refs_1_, bf16[1024,896]{1,0:T(8,128)(2,1)} %collective-permute-done.5.refs_2_, ...), custom_call_target="tpu_custom_call" | custom-call | flops 1 | bytes 1 | tf_op jit(solution)/shard_map/pallas_call | solution.py:109
  174.0 14.6 %shard_map.86 = (f32[1024,896]{1,0:T(8,128)}, f32[1024,896]{1,0:T(8,128)}) custom-call(s32[3]{0:T(128)} %add_add_fusion.1.order, bf16[1024,4096]{1,0:T(8,128)(2,1)} %all-gather.2.cloned.1.call-done.refs_0_, bf16[1024,896]{1,0:T(8,128)(2,1)} %get-tuple-element.49.refs_1_, bf16[1024,896]{1,0:T(8,128)(2,1)} %collective-permute-done.2.refs_2_, ...), custom_call_target="tpu_custom_call" | custom-call | flops 1 | bytes 1 | tf_op jit(solution)/shard_map/pallas_call | solution.py:109
  188.6 15.1 %shard_map.88 = (f32[1024,896]{1,0:T(8,128)}, f32[1024,896]{1,0:T(8,128)}) custom-call(s32[3]{0:T(128)} %add_add_fusion.order, bf16[1024,4096]{1,0:T(8,128)(2,1)} %all-gather.2.cloned.1.call-done.refs_0_, bf16[1024,896]{1,0:T(8,128)(2,1)} %collective-permute-done.4.refs_1_, bf16[1024,896]{1,0:T(8,128)(2,1)} %collective-permute-done.6.refs_2_, ...), custom_call_target="tpu_custom_call" | custom-call | flops 1 | bytes 1 | tf_op jit(solution)/shard_map/pallas_call | solution.py:109
  203.7 15.6 %shard_map.89 = (bf16[1024,896]{1,0:T(8,128)(2,1)}, bf16[1024,896]{1,0:T(8,128)(2,1)}) custom-call(s32[3]{0:T(128)} %add_add_fusion.order, bf16[1024,4096]{1,0:T(8,128)(2,1)} %all-gather.2.cloned.1.call-done.refs_0_, bf16[1024,896]{1,0:T(8,128)(2,1)} %collective-permute-done.1.refs_1_, bf16[1024,896]{1,0:T(8,128)(2,1)} %collective-permute-done.3.refs_2_, ...), custom_call_target="tpu_custom_call" | custom-call | flops 1 | bytes 1 | tf_op jit(solution)/shard_map/pallas_call | solution.py:109
  228.2 11.5 %shard_map.91 = (bf16[4,2,512,128]{3,2,1,0:T(8,128)(2,1)}, f32[4,2,512,128]{3,2,1,0:T(8,128)}) custom-call(s32[17]{0:T(128)} %stack.180.at, bf16[1024,896]{1,0:T(8,128)(2,1)} %get-tuple-element.33.refs_0_, bf16[1024,896]{1,0:T(8,128)(2,1)} %copy-done.1, bf16[1024,896]{1,0:T(8,128)(2,1)} %get-tuple-element.34.refs_2_, ...), custom_call_target="tpu_custom_call" | custom-call | flops 1 | bytes 1 | tf_op jit(solution)/shard_map/pallas_call | solution.py:151
  243.9 20.8 %collective-permute-done.14.refs_6_.refs_7_ = bf16[1792,256]{1,0:T(8,128)(2,1)S(1)} collective-permute-done((bf16[1792,256]{1,0:T(8,128)(2,1)}, bf16[1792,256]{1,0:T(8,128)(2,1)S(1)}, u32[]{:S(2)}, u32[]{:S(2)}) %collective-permute-start.14) | collective-permute-done | bytes 917536 | tf_op jit(solution)/shard_map/ppermute | solution.py:252
  265.6 11.8 %shard_map.92 = (bf16[4,2,512,128]{3,2,1,0:T(8,128)(2,1)}, f32[4,2,512,128]{3,2,1,0:T(8,128)}) custom-call(s32[17]{0:T(128)} %stack.194.at, bf16[1024,896]{1,0:T(8,128)(2,1)} %get-tuple-element.33.refs_0_, bf16[1024,896]{1,0:T(8,128)(2,1)} %copy-done.1, bf16[1024,896]{1,0:T(8,128)(2,1)} %get-tuple-element.34.refs_2_, ...), custom_call_target="tpu_custom_call" | custom-call | flops 1 | bytes 1 | tf_op jit(solution)/shard_map/pallas_call | solution.py:151
  277.4 5.8 %collective-permute-done.15.refs_2_.refs_6_.refs_7_ = bf16[1792,256]{1,0:T(8,128)(2,1)S(1)} collective-permute-done((bf16[1792,256]{1,0:T(8,128)(2,1)}, bf16[1792,256]{1,0:T(8,128)(2,1)S(1)}, u32[]{:S(2)}, u32[]{:S(2)}) %collective-permute-start.15) | collective-permute-done | bytes 917536 | tf_op jit(solution)/shard_map/ppermute | solution.py:252
  284.5 3.9 shard_map.93.refs_17_
  291.1 11.7 %shard_map.94 = (bf16[4,2,512,128]{3,2,1,0:T(8,128)(2,1)}, f32[4,2,512,128]{3,2,1,0:T(8,128)}) custom-call(s32[17]{0:T(128)} %stack.203.at, bf16[1024,896]{1,0:T(8,128)(2,1)} %get-tuple-element.33.refs_0_, bf16[1024,896]{1,0:T(8,128)(2,1)} %copy-done.1, bf16[1024,896]{1,0:T(8,128)(2,1)} %get-tuple-element.34.refs_2_, ...), custom_call_target="tpu_custom_call" | custom-call | flops 1 | bytes 1 | tf_op jit(solution)/shard_map/pallas_call | solution.py:151
  302.8 7.2 %collective-permute-done.17.refs_3_.refs_6_.refs_7_ = bf16[1792,256]{1,0:T(8,128)(2,1)S(1)} collective-permute-done((bf16[1792,256]{1,0:T(8,128)(2,1)S(1)}, bf16[1792,256]{1,0:T(8,128)(2,1)S(1)}, u32[]{:S(2)}, u32[]{:S(2)}) %collective-permute-start.17) | collective-permute-done | bytes 917536 | tf_op jit(solution)/shard_map/ppermute | solution.py:252
  315.9 3.9 shard_map.95.refs_17_
  322.1 11.7 %shard_map.96 = (bf16[4,2,512,128]{3,2,1,0:T(8,128)(2,1)}, f32[4,2,512,128]{3,2,1,0:T(8,128)}) custom-call(s32[17]{0:T(128)} %stack.212.at, bf16[1024,896]{1,0:T(8,128)(2,1)} %get-tuple-element.33.refs_0_, bf16[1024,896]{1,0:T(8,128)(2,1)} %copy-done.1, bf16[1024,896]{1,0:T(8,128)(2,1)} %get-tuple-element.34.refs_2_, ...), custom_call_target="tpu_custom_call" | custom-call | flops 1 | bytes 1 | tf_op jit(solution)/shard_map/pallas_call | solution.py:151
  333.8 11.0 %collective-permute-done.18.refs_0_ = bf16[4,2,512,128]{3,2,1,0:T(8,128)(2,1)S(1)} collective-permute-done((bf16[4,2,512,128]{3,2,1,0:T(8,128)(2,1)S(1)}, bf16[4,2,512,128]{3,2,1,0:T(8,128)(2,1)S(1)}, u32[]{:S(2)}, u32[]{:S(2)}) %collective-permute-start.18) | collective-permute-done | bytes 1048608 | tf_op jit(solution)/shard_map/ppermute | solution.py:325
  345.8 3.9 shard_map.97
  351.3 23.2 %collective-permute-done.19.refs_0_ = bf16[4,2,512,128]{3,2,1,0:T(8,128)(2,1)S(1)} collective-permute-done((bf16[4,2,512,128]{3,2,1,0:T(8,128)(2,1)S(1)}, bf16[4,2,512,128]{3,2,1,0:T(8,128)(2,1)S(1)}, u32[]{:S(2)}, u32[]{:S(2)}) %collective-permute-start.19) | collective-permute-done | bytes 1048608 | tf_op jit(solution)/shard_map/ppermute | solution.py:325
  375.7 3.9 shard_map.98
  379.6 26.0 %reduce-scatter.11.cloned.1.call-done = bf16[1,2,512,128]{3,2,1,0:T(8,128)(2,1)} async-done(((bf16[4,2,512,128]{3,2,1,0:T(8,128)(2,1)}), bf16[1,2,512,128]{3,2,1,0:T(8,128)(2,1)}) %reduce-scatter.11.cloned.1.call-update) | async-done | bytes 262160 | tf_op jit(solution)/shard_map/reduce_scatter | solution.py:330
  (115 shorter events, 66.4 us)
Async XLA Ops:
  7.2 152.4 %all-gather.2.cloned.1.call-start = ((), (), s32[]{:S(2)}) async-start(), calls=%async_computation.4 | async-start | bytes 9437184 | tf_op jit(solution)/shard_map/all_gather | solution.py:271
  7.2 15.2 %collective-permute-start = (bf16[512,512]{1,0:T(8,128)(2,1)}, bf16[512,512]{1,0:T(8,128)(2,1)S(1)}, u32[]{:S(2)}, u32[]{:S(2)}) collective-permute-start(bf16[512,512]{1,0:T(8,128)(2,1)} %param.7), channel_id=1, source_target_pairs={{0,16},{8,24},{16,0},{24,8},{1,17},{9,25},{17,1},{25,9},{2,18},{10... | collective-permute-start | bytes 1572872 | tf_op jit(solution)/shard_map/ppermute | solution.py:269
  23.5 292.4 %reduce-scatter.5.cloned.1.call-start = ((), (), s32[]{:S(2)}) async-start(), calls=%async_computation.5 | async-start | bytes 1310720 | tf_op jit(solution)/shard_map/reduce_scatter | solution.py:330
  26.4 43.1 %collective-permute-start.5 = (bf16[1024,896]{1,0:T(8,128)(2,1)}, bf16[1024,896]{1,0:T(8,128)(2,1)}, u32[]{:S(2)}, u32[]{:S(2)}) collective-permute-start(bf16[1024,896]{1,0:T(8,128)(2,1)} %get-tuple-element.46), channel_id=1, source_target_pairs={{0,16},{8,24},{16,0},{24,8},{1,17},{9,25},{17,1},{25,9},{2,18},{10... | collective-permute-start | bytes 5505032 | tf_op jit(solution)/shard_map/ppermute | solution.py:248
  28.2 80.7 %collective-permute-start.2 = (bf16[1024,896]{1,0:T(8,128)(2,1)}, bf16[1024,896]{1,0:T(8,128)(2,1)}, u32[]{:S(2)}, u32[]{:S(2)}) collective-permute-start(bf16[1024,896]{1,0:T(8,128)(2,1)} %get-tuple-element.48), channel_id=1, source_target_pairs={{0,16},{8,24},{16,0},{24,8},{1,17},{9,25},{17,1},{25,9},{2,18},{10... | collective-permute-start | bytes 5505032 | tf_op jit(solution)/shard_map/ppermute | solution.py:248
  33.5 114.2 %collective-permute-start.8 = (bf16[1792,512]{1,0:T(8,128)(2,1)}, bf16[1792,512]{1,0:T(8,128)(2,1)S(1)}, u32[]{:S(2)}, u32[]{:S(2)}) collective-permute-start(bf16[1792,512]{1,0:T(8,128)(2,1)} %pad_maximum_fusion.1), channel_id=1, source_target_pairs={{0,16},{8,24},{16,0},{24,8},{1,17},{9,25},{17,1},{25,9},{2,18},{10... | collective-permute-start | bytes 5505032 | tf_op jit(solution)/shard_map/ppermute | solution.py:267
  35.3 118.0 %collective-permute-start.4 = (bf16[1024,896]{1,0:T(8,128)(2,1)}, bf16[1024,896]{1,0:T(8,128)(2,1)}, u32[]{:S(2)}, u32[]{:S(2)}) collective-permute-start(bf16[1024,896]{1,0:T(8,128)(2,1)} %get-tuple-element.47.refs_1_), channel_id=1, source_target_pairs={{0,8},{8,0},{16,24},{24,16},{1,9},{9,1},{17,25},{25,17},{2,10},{10... | collective-permute-start | bytes 5505032 | tf_op jit(solution)/shard_map/ppermute | solution.py:252
  36.8 166.9 %collective-permute-start.1 = (bf16[1024,896]{1,0:T(8,128)(2,1)}, bf16[1024,896]{1,0:T(8,128)(2,1)}, u32[]{:S(2)}, u32[]{:S(2)}) collective-permute-start(bf16[1024,896]{1,0:T(8,128)(2,1)} %get-tuple-element.49.refs_1_), channel_id=1, source_target_pairs={{0,8},{8,0},{16,24},{24,16},{1,9},{9,1},{17,25},{25,17},{2,10},{10... | collective-permute-start | bytes 5505032 | tf_op jit(solution)/shard_map/ppermute | solution.py:252
  69.5 154.5 %collective-permute-start.12 = (bf16[896,2048]{1,0:T(8,128)(2,1)}, bf16[896,2048]{1,0:T(8,128)(2,1)}, u32[]{:S(2)}, u32[]{:S(2)}) collective-permute-start(bf16[896,2048]{1,0:T(8,128)(2,1)} %shard_map.90), channel_id=1, source_target_pairs={{0,1},{1,0},{2,3},{3,2},{4,5},{5,4},{6,7},{7,6},{8,9},{9,8},{10,11... | collective-permute-start | bytes 11010056 | tf_op jit(solution)/shard_map/ppermute | solution.py:280
  108.9 79.7 %collective-permute-start.6 = (bf16[1024,896]{1,0:T(8,128)(2,1)}, bf16[1024,896]{1,0:T(8,128)(2,1)}, u32[]{:S(2)}, u32[]{:S(2)}) collective-permute-start(bf16[1024,896]{1,0:T(8,128)(2,1)} %collective-permute-done.5.refs_2_), channel_id=1, source_target_pairs={{0,8},{8,0},{16,24},{24,16},{1,9},{9,1},{17,25},{25,17},{2,10},{10... | collective-permute-start | bytes 5505032 | tf_op jit(solution)/shard_map/ppermute | solution.py:252
  147.7 56.0 %collective-permute-start.3 = (bf16[1024,896]{1,0:T(8,128)(2,1)}, bf16[1024,896]{1,0:T(8,128)(2,1)}, u32[]{:S(2)}, u32[]{:S(2)}) collective-permute-start(bf16[1024,896]{1,0:T(8,128)(2,1)} %collective-permute-done.2.refs_2_), channel_id=1, source_target_pairs={{0,8},{8,0},{16,24},{24,16},{1,9},{9,1},{17,25},{25,17},{2,10},{10... | collective-permute-start | bytes 5505032 | tf_op jit(solution)/shard_map/ppermute | solution.py:252
  153.3 66.0 %collective-permute-start.9 = (bf16[1792,256]{1,0:T(8,128)(2,1)S(1)}, bf16[1792,256]{1,0:T(8,128)(2,1)S(1)}, u32[]{:S(2)}, u32[]{:S(2)}) collective-permute-start(bf16[1792,256]{1,0:T(8,128)(2,1)S(1)} %pad_maximum_fusion.4.refs_8_), channel_id=1, source_target_pairs={{0,8},{8,0},{16,24},{24,16},{1,9},{9,1},{17,25},{25,17},{2,10},{10... | collective-permute-start | bytes 2752520 | tf_op jit(solution)/shard_map/ppermute | solution.py:252
  220.3 6.6 %collective-permute-start.10 = (bf16[1024,896]{1,0:T(8,128)(2,1)}, bf16[1024,896]{1,0:T(8,128)(2,1)S(1)}, u32[]{:S(2)}, u32[]{:S(2)}) collective-permute-start(bf16[1024,896]{1,0:T(8,128)(2,1)} %get-tuple-element.33.refs_0_), channel_id=1, source_target_pairs={{0,1},{1,0},{2,3},{3,2},{4,5},{5,4},{6,7},{7,6},{8,9},{9,8},{10,11... | collective-permute-start | bytes 5505032 | tf_op jit(solution)/shard_map/ppermute | solution.py:308
  220.3 6.7 %collective-permute-start.11 = (bf16[1024,896]{1,0:T(8,128)(2,1)}, bf16[1024,896]{1,0:T(8,128)(2,1)}, u32[]{:S(2)}, u32[]{:S(2)}) collective-permute-start(bf16[1024,896]{1,0:T(8,128)(2,1)} %get-tuple-element.34.refs_2_), channel_id=1, source_target_pairs={{0,1},{1,0},{2,3},{3,2},{4,5},{5,4},{6,7},{7,6},{8,9},{9,8},{10,11... | collective-permute-start | bytes 5505032 | tf_op jit(solution)/shard_map/ppermute | solution.py:308
  239.7 43.5 %collective-permute-start.13 = (bf16[4,2,512,128]{3,2,1,0:T(8,128)(2,1)}, bf16[4,2,512,128]{3,2,1,0:T(8,128)(2,1)S(1)}, u32[]{:S(2)}, u32[]{:S(2)}) collective-permute-start(bf16[4,2,512,128]{3,2,1,0:T(8,128)(2,1)} %get-tuple-element.37.refs_16_), channel_id=1, source_target_pairs={{0,16},{8,24},{16,0},{24,8},{1,17},{9,25},{17,1},{25,9},{2,18},{10... | collective-permute-start | bytes 3145736 | tf_op jit(solution)/shard_map/ppermute | solution.py:325
  241.2 23.5 %collective-permute-start.14 = (bf16[1792,256]{1,0:T(8,128)(2,1)}, bf16[1792,256]{1,0:T(8,128)(2,1)S(1)}, u32[]{:S(2)}, u32[]{:S(2)}) collective-permute-start(bf16[1792,256]{1,0:T(8,128)(2,1)} %pad_maximum_fusion.5.refs_9_), channel_id=1, source_target_pairs={{0,8},{8,0},{16,24},{24,16},{1,9},{9,1},{17,25},{25,17},{2,10},{10... | collective-permute-start | bytes 2752520 | tf_op jit(solution)/shard_map/ppermute | solution.py:252
  242.6 40.6 %collective-permute-start.15 = (bf16[1792,256]{1,0:T(8,128)(2,1)}, bf16[1792,256]{1,0:T(8,128)(2,1)S(1)}, u32[]{:S(2)}, u32[]{:S(2)}) collective-permute-start(bf16[1792,256]{1,0:T(8,128)(2,1)} %pad_maximum_fusion.6.refs_10_), channel_id=1, source_target_pairs={{0,8},{8,0},{16,24},{24,16},{1,9},{9,1},{17,25},{25,17},{2,10},{10... | collective-permute-start | bytes 2752520 | tf_op jit(solution)/shard_map/ppermute | solution.py:252
  288.4 57.4 %reduce-scatter.7.cloned.1.call-start = ((), (), s32[]{:S(2)}) async-start(), calls=%async_computation.6 | async-start | bytes 1310720 | tf_op jit(solution)/shard_map/reduce_scatter | solution.py:330
  288.5 24.2 %collective-permute-start.16 = (bf16[4,2,512,128]{3,2,1,0:T(8,128)(2,1)S(1)}, bf16[4,2,512,128]{3,2,1,0:T(8,128)(2,1)}, u32[]{:S(2)}, u32[]{:S(2)}) collective-permute-start(bf16[4,2,512,128]{3,2,1,0:T(8,128)(2,1)S(1)} %copy-done.5), channel_id=1, source_target_pairs={{0,16},{8,24},{16,0},{24,8},{1,17},{9,25},{17,1},{25,9},{2,18},{10... | collective-permute-start | bytes 3145736 | tf_op jit(solution)/shard_map/ppermute | solution.py:325
  289.1 21.0 %collective-permute-start.17 = (bf16[1792,256]{1,0:T(8,128)(2,1)S(1)}, bf16[1792,256]{1,0:T(8,128)(2,1)S(1)}, u32[]{:S(2)}, u32[]{:S(2)}) collective-permute-start(bf16[1792,256]{1,0:T(8,128)(2,1)S(1)} %copy-done.10), channel_id=1, source_target_pairs={{0,8},{8,0},{16,24},{24,16},{1,9},{9,1},{17,25},{25,17},{2,10},{10... | collective-permute-start | bytes 2752520 | tf_op jit(solution)/shard_map/ppermute | solution.py:252
  319.8 55.9 %reduce-scatter.9.cloned.1.call-start = ((), (), s32[]{:S(2)}) async-start(), calls=%async_computation.7 | async-start | bytes 1310720 | tf_op jit(solution)/shard_map/reduce_scatter | solution.py:330
  319.9 24.8 %collective-permute-start.18 = (bf16[4,2,512,128]{3,2,1,0:T(8,128)(2,1)S(1)}, bf16[4,2,512,128]{3,2,1,0:T(8,128)(2,1)S(1)}, u32[]{:S(2)}, u32[]{:S(2)}) collective-permute-start(bf16[4,2,512,128]{3,2,1,0:T(8,128)(2,1)S(1)} %copy-done.4), channel_id=1, source_target_pairs={{0,16},{8,24},{16,0},{24,8},{1,17},{9,25},{17,1},{25,9},{2,18},{10... | collective-permute-start | bytes 3145736 | tf_op jit(solution)/shard_map/ppermute | solution.py:325
  349.7 55.9 %reduce-scatter.11.cloned.1.call-start = ((), (), s32[]{:S(2)}) async-start(), calls=%async_computation.8 | async-start | bytes 1310720 | tf_op jit(solution)/shard_map/reduce_scatter | solution.py:330
  349.8 24.8 %collective-permute-start.19 = (bf16[4,2,512,128]{3,2,1,0:T(8,128)(2,1)S(1)}, bf16[4,2,512,128]{3,2,1,0:T(8,128)(2,1)S(1)}, u32[]{:S(2)}, u32[]{:S(2)}) collective-permute-start(bf16[4,2,512,128]{3,2,1,0:T(8,128)(2,1)S(1)} %copy-done.6), channel_id=1, source_target_pairs={{0,16},{8,24},{16,0},{24,8},{1,17},{9,25},{17,1},{25,9},{2,18},{10... | collective-permute-start | bytes 3145736 | tf_op jit(solution)/shard_map/ppermute | solution.py:325
  (23 other events, 155.1 us)
Sparse Core Ops, SparseCore 0:
  23.6 83.5 all-gather.1
  288.5 27.3 reduce-scatter.4
  320.0 25.8 reduce-scatter.6
  349.8 25.8 reduce-scatter.8
  379.8 25.8 reduce-scatter.10

commit v2 on v1

--- a/solution.py
+++ b/solution.py
@@ -197,27 +197,6 @@
     )(jnp.stack([y, h]).astype(jnp.int32), previous)
 
 
-def add_kernel(n_after, keep, *refs):
-    *got, out = refs[: len(refs) - 1 - n_after] + refs[-1:]
-    total = keep[...]
-    for v in got:
-        total = total + v[...].astype(jnp.float32)
-    out[...] = total.astype(out.dtype)
-
-
-def add_all(keep, got, after):
-    block = pl.BlockSpec((1, *keep.shape[1:]), lambda q: (q, 0, 0, 0))
-    return pl.pallas_call(
-        functools.partial(add_kernel, len(after)),
-        grid=(keep.shape[0],),
-        in_specs=[block] * (1 + len(got)) + [pl.BlockSpec(memory_space=pl.ANY)] * len(after),
-        out_specs=block,
-        out_shape=jax.ShapeDtypeStruct(keep.shape, jnp.bfloat16),
-        compiler_params=pltpu.CompilerParams(vmem_limit_bytes=VMEM_BYTES),
-        cost_estimate=CHEAP,
-    )(keep, *got, *after)
-
-
 def make_local(n_dp, n_mp):
     ny, nz = n_dp // 2, n_mp // 2
     assert nz == n_dp and n_dp % 2 == 0
@@ -253,8 +232,12 @@
 
         gate_near = swap_units(gate_on, 1)
         up_near = swap_units(up_on, 1)
+        gate_far, up_far = from_x(gate_near), from_x(up_near)
         cols = down_on.shape[1]
         half = cols // 2
+        (down_on, down_prev), _ = lax.optimization_barrier(
+            ((down_on, down_prev), (gate_near[1:], up_near[1:], gate_far[0], up_far[0]))
+        )
         down_mine = lax.dynamic_slice_in_dim(down_on, c * half, half, 1)
         down_give = lax.dynamic_slice_in_dim(down_on, (1 - c) * half, half, 1)
         down_pairs = [down_mine, lax.ppermute(down_give, "mp", along_core)]
@@ -265,7 +248,6 @@
                 [lax.dynamic_slice_in_dim(w, start, own_units, 0) for w in down_pairs], 0
             )
             down_near.append(piece if r == 0 else lax.ppermute(piece, "dp", along_y(r)))
-        gate_far, up_far = from_x(gate_near), from_x(up_near)
         mine = [hidden] + [lax.ppermute(hidden, "dp", along_y(r)) for r in range(1, ny)]
         mine, *_ = lax.optimization_barrier((mine, gate_near[0], up_near[0]))
         features = lax.all_gather(jnp.concatenate(mine, 0), "mp", axis=1, tiled=True)
@@ -281,6 +263,8 @@
 
         gate_part = hidden_pair(features, [*near, first], gate_near, gate_old)
         up_part = hidden_pair(features, [*near, first], up_near, up_old)
+        down_near, _ = lax.optimization_barrier((down_near, (gate_part, up_part)))
+
         step = 128
         jobs = half // step
         down_send = [
@@ -297,7 +281,7 @@
             up_old,
             start=up_part,
             gates=gates,
-            after=down_send,
+            after=down_send + down_near,
         )
 
         (inner_o, inner_t), down_far[0] = lax.optimization_barrier(
@@ -321,12 +305,18 @@
                 ny,
                 after,
             )
+            if s + 1 < jobs:
+                gives, down_far[s + 1] = lax.optimization_barrier((gives, down_far[s + 1]))
             return keep, gives, [
                 lax.ppermute(v, "dp", along_y(ny - 1 - r)) for r, v in enumerate(gives)
             ]
 
-        def over_z(keep, from_y, earlier):
-            total = add_all(keep, from_y, earlier)
+        def over_z(keep, from_y, after, earlier):
+            (keep, from_y), _ = lax.optimization_barrier(((keep, from_y), after))
+            total = keep
+            for v in from_y:
+                total = total + v.astype(jnp.float32)
+            total, _ = lax.optimization_barrier((total.astype(jnp.bfloat16), earlier))
             summed = lax.psum_scatter(
                 total, "mp", scatter_dimension=0, axis_index_groups=same_core, tiled=True
             )
@@ -339,10 +329,7 @@
                 keep, gives, from_y = products(s, last + total)
                 last = gives[:1]
             if waiting is not None:
-                ahead = last + results[-1:]
-                if s + 1 < jobs:
-                    ahead.append(down_far[s + 1])
-                total, summed = over_z(*waiting, ahead)
+                total, summed = over_z(*waiting, last, results[-1:])
                 total = [total]
                 results.append(summed)
             waiting = keep, from_y

time: 418 us -> 393 us (0.940)
  Pallas kernels: 127 us -> 112 us
  waiting for transfers between devices: 213 us -> 202 us
    ppermute x8, waiting for transfers between devices: 33.8 us -> 113 us  [from_x(): return [lax.ppermute(p, 'dp', along_x) for p in pieces]]
    ppermute x2, waiting for transfers between devices: 65.3 us -> 3.5 us  [swap_units(): out.append(piece if r == 0 else lax.ppermute(piece, 'dp', along_y(r)))]
    ppermute x1, waiting for transfers between devices: 37.1 us -> 1.71 us  [local(): down_near.append(piece if r == 0 else lax.ppermute(piece, 'dp', along_y(r)))]
    pallas_call x4 -> x0, Pallas kernels: 15.6 us -> none  [add_all(): pl.pallas_call(functools.partial(add_kernel, len(after)), grid=(keep.shap...]
    convert_element_type x0 -> x4, other arithmetic: none -> 7.58 us  [over_z(): total, _ = lax.optimization_barrier((total.astype(jnp.bfloat16), earlier))]
  transfers between devices with their start and end apart: 25 -> 25, of which waited for: 16 -> 22; matrix products, arithmetic and copies ran while one was open for 7% -> 8% of each run, Pallas kernels for 24% -> 29%
where the time goes in v2:
time: 393 us; the launch traced here: 390 us
  waiting for transfers between devices  202 us (51%)
  Pallas kernels  112 us (28%)
  starting transfers between devices  21.6 us (5%)
  local copies, waits for them, and re-layouts  21.6 us (5%)
  other arithmetic  17.5 us (4%)
  between operations  14.4 us (4%)
    ppermute x8, waiting for transfers between devices, from_x(): return [lax.ppermute(p, 'dp', along_x) for p in pieces]  113 us
    pallas_call x4, Pallas kernels, hidden_pair(): pl.pallas_call(functools.partial(hidden_kernel, n, len(start), len(gates)...  59.8 us
    pallas_call x4, Pallas kernels, down_pair(): pl.pallas_call(functools.partial(down_kernel, n, ny, len(after)), grid_sp...  46.7 us
    ppermute x4, waiting for transfers between devices, products(): lax.ppermute(v, 'dp', along_y(ny - 1 - r))  39.5 us
    reduce_scatter x4, waiting for transfers between devices, over_z(): lax.psum_scatter(total, 'mp', scatter_dimension=0, axis_index_groups=same...  33.3 us
    ppermute x8, starting transfers between devices, from_x(): return [lax.ppermute(p, 'dp', along_x) for p in pieces]  10 us
  transfers between devices with their start and end apart: 25, of which 22 were waited for; matrix products, arithmetic and copies ran while one was open for 8% of the time, Pallas kernels for 29%

profile of v2, /device:TPU:0, one launch (start us, length us, event | category | flops | bytes accessed | tf_op | source)
XLA Modules:
  0.0 389.7 jit_solution(5675989763692771284)
XLA Ops:
  7.2 3.0 collective-permute-start
  10.2 3.8 constant_dynamic-slice_fusion.3
  16.2 6.2 %collective-permute-done = bf16[512,512]{1,0:T(8,128)(2,1)S(1)} collective-permute-done((bf16[512,512]{1,0:T(8,128)(2,1)}, bf16[512,512]{1,0:T(8,128)(2,1)S(1)}, u32[]{:S(2)}, u32[]{:S(2)}) %collective-permute-start) | collective-permute-done | bytes 524320 | tf_op jit(solution)/shard_map/ppermute | solution.py:251
  27.7 39.2 %collective-permute-done.1.refs_1_ = bf16[1024,896]{1,0:T(8,128)(2,1)} collective-permute-done((bf16[1024,896]{1,0:T(8,128)(2,1)}, bf16[1024,896]{1,0:T(8,128)(2,1)}, u32[]{:S(2)}, u32[]{:S(2)}) %collective-permute-start.1) | collective-permute-done | bytes 1835040 | tf_op jit(solution)/shard_map/ppermute | solution.py:231
  68.9 35.5 %collective-permute-done.4.refs_1_ = bf16[1024,896]{1,0:T(8,128)(2,1)} collective-permute-done((bf16[1024,896]{1,0:T(8,128)(2,1)S(1)}, bf16[1024,896]{1,0:T(8,128)(2,1)}, u32[]{:S(2)}, u32[]{:S(2)}) %collective-permute-start.4) | collective-permute-done | bytes 1835040 | tf_op jit(solution)/shard_map/ppermute | solution.py:231
  105.9 2.9 constant_dynamic-slice_fusion.2
  119.3 5.6 %shard_map.90 = bf16[896,2048]{1,0:T(8,128)(2,1)} custom-call(s32[2]{0:T(128)} %pad_add_fusion.at, bf16[1792,4096]{1,0:T(8,128)(2,1)} %refs_11_.3), custom_call_target="tpu_custom_call" | custom-call | flops 1 | bytes 1 | tf_op jit(solution)/shard_map/pallas_call | solution.py:187
  127.0 14.3 %shard_map.86 = (f32[1024,896]{1,0:T(8,128)}, f32[1024,896]{1,0:T(8,128)}) custom-call(s32[3]{0:T(128)} %add_add_fusion.1.order, bf16[1024,4096]{1,0:T(8,128)(2,1)} %all-gather.2.cloned.1.call-done.refs_0_, bf16[1024,896]{1,0:T(8,128)(2,1)} %get-tuple-element.91.refs_1_, bf16[1024,896]{1,0:T(8,128)(2,1)} %collective-permute-done.2.refs_2_, ...), custom_call_target="tpu_custom_call" | custom-call | flops 1 | bytes 1 | tf_op jit(solution)/shard_map/pallas_call | solution.py:109
  141.3 14.6 %shard_map.87 = (f32[1024,896]{1,0:T(8,128)}, f32[1024,896]{1,0:T(8,128)}) custom-call(s32[3]{0:T(128)} %add_add_fusion.1.order, bf16[1024,4096]{1,0:T(8,128)(2,1)} %all-gather.2.cloned.1.call-done.refs_0_, bf16[1024,896]{1,0:T(8,128)(2,1)} %copy-done.2, bf16[1024,896]{1,0:T(8,128)(2,1)} %collective-permute-done.5.refs_2_, bf16[4096,1792]{1,0:T(8,128)(2,1)} %refs_3_.6), custom_call_target="tpu_custom_call" | custom-call | flops 1 | bytes 1 | tf_op jit(solution)/shard_map/pallas_call | solution.py:109
  157.6 3.0 fusion.1
  162.8 15.2 %shard_map.88 = (f32[1024,896]{1,0:T(8,128)}, f32[1024,896]{1,0:T(8,128)}) custom-call(s32[3]{0:T(128)} %add_add_fusion.order, bf16[1024,4096]{1,0:T(8,128)(2,1)} %all-gather.2.cloned.1.call-done.refs_0_, bf16[1024,896]{1,0:T(8,128)(2,1)} %collective-permute-done.4.refs_1_, bf16[1024,896]{1,0:T(8,128)(2,1)} %collective-permute-done.6.refs_2_, ...), custom_call_target="tpu_custom_call" | custom-call | flops 1 | bytes 1 | tf_op jit(solution)/shard_map/pallas_call | solution.py:109
  181.6 17.6 %collective-permute-done.3.refs_2_ = bf16[1024,896]{1,0:T(8,128)(2,1)} collective-permute-done((bf16[1024,896]{1,0:T(8,128)(2,1)}, bf16[1024,896]{1,0:T(8,128)(2,1)}, u32[]{:S(2)}, u32[]{:S(2)}) %collective-permute-start.3) | collective-permute-done | bytes 1835040 | tf_op jit(solution)/shard_map/ppermute | solution.py:231
  199.2 15.6 %shard_map.89 = (bf16[1024,896]{1,0:T(8,128)(2,1)}, bf16[1024,896]{1,0:T(8,128)(2,1)}) custom-call(s32[3]{0:T(128)} %add_add_fusion.order, bf16[1024,4096]{1,0:T(8,128)(2,1)} %all-gather.2.cloned.1.call-done.refs_0_, bf16[1024,896]{1,0:T(8,128)(2,1)} %collective-permute-done.1.refs_1_, bf16[1024,896]{1,0:T(8,128)(2,1)} %collective-permute-done.3.refs_2_, ...), custom_call_target="tpu_custom_call" | custom-call | flops 1 | bytes 1 | tf_op jit(solution)/shard_map/pallas_call | solution.py:109
  220.3 3.9 %collective-permute-done.10.refs_1_ = bf16[1024,896]{1,0:T(8,128)(2,1)S(1)} collective-permute-done((bf16[1024,896]{1,0:T(8,128)(2,1)}, bf16[1024,896]{1,0:T(8,128)(2,1)S(1)}, u32[]{:S(2)}, u32[]{:S(2)}) %collective-permute-start.10) | collective-permute-done | bytes 1835040 | tf_op jit(solution)/shard_map/ppermute | solution.py:292
  225.5 11.4 %shard_map.91 = (bf16[4,2,512,128]{3,2,1,0:T(8,128)(2,1)}, f32[4,2,512,128]{3,2,1,0:T(8,128)}) custom-call(s32[17]{0:T(128)} %stack.180.at, bf16[1024,896]{1,0:T(8,128)(2,1)} %get-tuple-element.57.refs_0_, bf16[1024,896]{1,0:T(8,128)(2,1)} %copy-done.1, bf16[1024,896]{1,0:T(8,128)(2,1)} %get-tuple-element.58.refs_2_, ...), custom_call_target="tpu_custom_call" | custom-call | flops 1 | bytes 1 | tf_op jit(solution)/shard_map/pallas_call | solution.py:151
  236.9 3.8 collective-permute-done.13.refs_6_.refs_7_
  243.4 11.8 %shard_map.92 = (bf16[4,2,512,128]{3,2,1,0:T(8,128)(2,1)}, f32[4,2,512,128]{3,2,1,0:T(8,128)}) custom-call(s32[17]{0:T(128)} %stack.194.at, bf16[1024,896]{1,0:T(8,128)(2,1)} %get-tuple-element.57.refs_0_, bf16[1024,896]{1,0:T(8,128)(2,1)} %copy-done.1, bf16[1024,896]{1,0:T(8,128)(2,1)} %get-tuple-element.58.refs_2_, ...), custom_call_target="tpu_custom_call" | custom-call | flops 1 | bytes 1 | tf_op jit(solution)/shard_map/pallas_call | solution.py:151
  255.2 7.4 %collective-permute-done.15.refs_6_.refs_7_ = bf16[1792,256]{1,0:T(8,128)(2,1)S(1)} collective-permute-done((bf16[1792,256]{1,0:T(8,128)(2,1)}, bf16[1792,256]{1,0:T(8,128)(2,1)S(1)}, u32[]{:S(2)}, u32[]{:S(2)}) %collective-permute-start.15) | collective-permute-done | bytes 917536 | tf_op jit(solution)/shard_map/ppermute | solution.py:231
  271.6 11.8 %shard_map.93 = (bf16[4,2,512,128]{3,2,1,0:T(8,128)(2,1)}, f32[4,2,512,128]{3,2,1,0:T(8,128)}) custom-call(s32[17]{0:T(128)} %stack.203.at, bf16[1024,896]{1,0:T(8,128)(2,1)} %get-tuple-element.57.refs_0_, bf16[1024,896]{1,0:T(8,128)(2,1)} %copy-done.1, bf16[1024,896]{1,0:T(8,128)(2,1)} %get-tuple-element.58.refs_2_, ...), custom_call_target="tpu_custom_call" | custom-call | flops 1 | bytes 1 | tf_op jit(solution)/shard_map/pallas_call | solution.py:151
  283.4 6.3 %collective-permute-done.17.refs_6_.refs_7_ = bf16[1792,256]{1,0:T(8,128)(2,1)S(1)} collective-permute-done((bf16[1792,256]{1,0:T(8,128)(2,1)S(1)}, bf16[1792,256]{1,0:T(8,128)(2,1)S(1)}, u32[]{:S(2)}, u32[]{:S(2)}) %collective-permute-start.17) | collective-permute-done | bytes 917536 | tf_op jit(solution)/shard_map/ppermute | solution.py:231
  298.5 11.7 %shard_map.94 = (bf16[4,2,512,128]{3,2,1,0:T(8,128)(2,1)}, f32[4,2,512,128]{3,2,1,0:T(8,128)}) custom-call(s32[17]{0:T(128)} %stack.212.at, bf16[1024,896]{1,0:T(8,128)(2,1)} %get-tuple-element.57.refs_0_, bf16[1024,896]{1,0:T(8,128)(2,1)} %copy-done.1, bf16[1024,896]{1,0:T(8,128)(2,1)} %get-tuple-element.58.refs_2_, ...), custom_call_target="tpu_custom_call" | custom-call | flops 1 | bytes 1 | tf_op jit(solution)/shard_map/pallas_call | solution.py:151
  310.2 10.9 %collective-permute-done.18 = bf16[4,2,512,128]{3,2,1,0:T(8,128)(2,1)S(1)} collective-permute-done((bf16[4,2,512,128]{3,2,1,0:T(8,128)(2,1)S(1)}, bf16[4,2,512,128]{3,2,1,0:T(8,128)(2,1)S(1)}, u32[]{:S(2)}, u32[]{:S(2)}) %collective-permute-start.18) | collective-permute-done | bytes 1048608 | tf_op jit(solution)/shard_map/ppermute | solution.py:311
  326.1 23.5 %collective-permute-done.19 = bf16[4,2,512,128]{3,2,1,0:T(8,128)(2,1)S(1)} collective-permute-done((bf16[4,2,512,128]{3,2,1,0:T(8,128)(2,1)}, bf16[4,2,512,128]{3,2,1,0:T(8,128)(2,1)S(1)}, u32[]{:S(2)}, u32[]{:S(2)}) %collective-permute-start.19) | collective-permute-done | bytes 1048608 | tf_op jit(solution)/shard_map/ppermute | solution.py:311
  352.5 28.0 %reduce-scatter.11.cloned.1.call-done = bf16[1,2,512,128]{3,2,1,0:T(8,128)(2,1)} async-done(((bf16[4,2,512,128]{3,2,1,0:T(8,128)(2,1)}), bf16[1,2,512,128]{3,2,1,0:T(8,128)(2,1)}) %reduce-scatter.11.cloned.1.call-update) | async-done | bytes 262160 | tf_op jit(solution)/shard_map/reduce_scatter | solution.py:320
  (118 shorter events, 68.0 us)
Async XLA Ops:
  7.2 119.8 %all-gather.2.cloned.1.call-start = ((), (), s32[]{:S(2)}) async-start(), calls=%async_computation.4 | async-start | bytes 9437184 | tf_op jit(solution)/shard_map/all_gather | solution.py:253
  7.2 15.2 %collective-permute-start = (bf16[512,512]{1,0:T(8,128)(2,1)}, bf16[512,512]{1,0:T(8,128)(2,1)S(1)}, u32[]{:S(2)}, u32[]{:S(2)}) collective-permute-start(bf16[512,512]{1,0:T(8,128)(2,1)} %param.7), channel_id=1, source_target_pairs={{0,16},{8,24},{16,0},{24,8},{1,17},{9,25},{17,1},{25,9},{2,18},{10... | collective-permute-start | bytes 1572872 | tf_op jit(solution)/shard_map/ppermute | solution.py:251
  23.5 272.8 %reduce-scatter.5.cloned.1.call-start = ((), (), s32[]{:S(2)}) async-start(), calls=%async_computation.5 | async-start | bytes 1310720 | tf_op jit(solution)/shard_map/reduce_scatter | solution.py:320
  23.5 43.3 %collective-permute-start.1 = (bf16[1024,896]{1,0:T(8,128)(2,1)}, bf16[1024,896]{1,0:T(8,128)(2,1)}, u32[]{:S(2)}, u32[]{:S(2)}) collective-permute-start(bf16[1024,896]{1,0:T(8,128)(2,1)} %get-tuple-element.91.refs_1_), channel_id=1, source_target_pairs={{0,8},{8,0},{16,24},{24,16},{1,9},{9,1},{17,25},{25,17},{2,10},{10... | collective-permute-start | bytes 5505032 | tf_op jit(solution)/shard_map/ppermute | solution.py:231
  25.3 79.1 %collective-permute-start.4 = (bf16[1024,896]{1,0:T(8,128)(2,1)S(1)}, bf16[1024,896]{1,0:T(8,128)(2,1)}, u32[]{:S(2)}, u32[]{:S(2)}) collective-permute-start(bf16[1024,896]{1,0:T(8,128)(2,1)S(1)} %get-tuple-element.89.refs_1_), channel_id=1, source_target_pairs={{0,8},{8,0},{16,24},{24,16},{1,9},{9,1},{17,25},{25,17},{2,10},{10... | collective-permute-start | bytes 5505032 | tf_op jit(solution)/shard_map/ppermute | solution.py:231
  25.6 43.3 %collective-permute-start.2 = (bf16[1024,896]{1,0:T(8,128)(2,1)}, bf16[1024,896]{1,0:T(8,128)(2,1)}, u32[]{:S(2)}, u32[]{:S(2)}) collective-permute-start(bf16[1024,896]{1,0:T(8,128)(2,1)} %get-tuple-element.90), channel_id=1, source_target_pairs={{0,16},{8,24},{16,0},{24,8},{1,17},{9,25},{17,1},{25,9},{2,18},{10... | collective-permute-start | bytes 5505032 | tf_op jit(solution)/shard_map/ppermute | solution.py:227
  27.4 78.5 %collective-permute-start.5 = (bf16[1024,896]{1,0:T(8,128)(2,1)}, bf16[1024,896]{1,0:T(8,128)(2,1)}, u32[]{:S(2)}, u32[]{:S(2)}) collective-permute-start(bf16[1024,896]{1,0:T(8,128)(2,1)} %get-tuple-element.88), channel_id=1, source_target_pairs={{0,16},{8,24},{16,0},{24,8},{1,17},{9,25},{17,1},{25,9},{2,18},{10... | collective-permute-start | bytes 5505032 | tf_op jit(solution)/shard_map/ppermute | solution.py:227
  115.2 42.4 %collective-permute-start.8 = (bf16[1792,512]{1,0:T(8,128)(2,1)}, bf16[1792,512]{1,0:T(8,128)(2,1)}, u32[]{:S(2)}, u32[]{:S(2)}) collective-permute-start(bf16[1792,512]{1,0:T(8,128)(2,1)} %pad_maximum_fusion.1), channel_id=1, source_target_pairs={{0,16},{8,24},{16,0},{24,8},{1,17},{9,25},{17,1},{25,9},{2,18},{10... | collective-permute-start | bytes 5505032 | tf_op jit(solution)/shard_map/ppermute | solution.py:250
  116.7 46.1 %collective-permute-start.6 = (bf16[1024,896]{1,0:T(8,128)(2,1)}, bf16[1024,896]{1,0:T(8,128)(2,1)}, u32[]{:S(2)}, u32[]{:S(2)}) collective-permute-start(bf16[1024,896]{1,0:T(8,128)(2,1)} %collective-permute-done.5.refs_2_), channel_id=1, source_target_pairs={{0,8},{8,0},{16,24},{24,16},{1,9},{9,1},{17,25},{25,17},{2,10},{10... | collective-permute-start | bytes 5505032 | tf_op jit(solution)/shard_map/ppermute | solution.py:231
  124.9 95.3 %collective-permute-start.12 = (bf16[896,2048]{1,0:T(8,128)(2,1)}, bf16[896,2048]{1,0:T(8,128)(2,1)}, u32[]{:S(2)}, u32[]{:S(2)}) collective-permute-start(bf16[896,2048]{1,0:T(8,128)(2,1)} %shard_map.90), channel_id=1, source_target_pairs={{0,1},{1,0},{2,3},{3,2},{4,5},{5,4},{6,7},{7,6},{8,9},{9,8},{10,11... | collective-permute-start | bytes 11010056 | tf_op jit(solution)/shard_map/ppermute | solution.py:262
  125.0 74.2 %collective-permute-start.3 = (bf16[1024,896]{1,0:T(8,128)(2,1)}, bf16[1024,896]{1,0:T(8,128)(2,1)}, u32[]{:S(2)}, u32[]{:S(2)}) collective-permute-start(bf16[1024,896]{1,0:T(8,128)(2,1)} %collective-permute-done.2.refs_2_), channel_id=1, source_target_pairs={{0,8},{8,0},{16,24},{24,16},{1,9},{9,1},{17,25},{25,17},{2,10},{10... | collective-permute-start | bytes 5505032 | tf_op jit(solution)/shard_map/ppermute | solution.py:231
  160.7 56.9 %collective-permute-start.9 = (bf16[1792,256]{1,0:T(8,128)(2,1)S(1)}, bf16[1792,256]{1,0:T(8,128)(2,1)S(1)}, u32[]{:S(2)}, u32[]{:S(2)}) collective-permute-start(bf16[1792,256]{1,0:T(8,128)(2,1)S(1)} %pad_maximum_fusion.4.refs_8_), channel_id=1, source_target_pairs={{0,8},{8,0},{16,24},{24,16},{1,9},{9,1},{17,25},{25,17},{2,10},{10... | collective-permute-start | bytes 2752520 | tf_op jit(solution)/shard_map/ppermute | solution.py:231
  217.6 6.6 %collective-permute-start.10 = (bf16[1024,896]{1,0:T(8,128)(2,1)}, bf16[1024,896]{1,0:T(8,128)(2,1)S(1)}, u32[]{:S(2)}, u32[]{:S(2)}) collective-permute-start(bf16[1024,896]{1,0:T(8,128)(2,1)} %get-tuple-element.57.refs_0_), channel_id=1, source_target_pairs={{0,1},{1,0},{2,3},{3,2},{4,5},{5,4},{6,7},{7,6},{8,9},{9,8},{10,11... | collective-permute-start | bytes 5505032 | tf_op jit(solution)/shard_map/ppermute | solution.py:292
  217.6 6.7 %collective-permute-start.11 = (bf16[1024,896]{1,0:T(8,128)(2,1)}, bf16[1024,896]{1,0:T(8,128)(2,1)}, u32[]{:S(2)}, u32[]{:S(2)}) collective-permute-start(bf16[1024,896]{1,0:T(8,128)(2,1)} %get-tuple-element.58.refs_2_), channel_id=1, source_target_pairs={{0,1},{1,0},{2,3},{3,2},{4,5},{5,4},{6,7},{7,6},{8,9},{9,8},{10,11... | collective-permute-start | bytes 5505032 | tf_op jit(solution)/shard_map/ppermute | solution.py:292
  218.2 22.6 %collective-permute-start.13 = (bf16[1792,256]{1,0:T(8,128)(2,1)}, bf16[1792,256]{1,0:T(8,128)(2,1)}, u32[]{:S(2)}, u32[]{:S(2)}) collective-permute-start(bf16[1792,256]{1,0:T(8,128)(2,1)} %pad_maximum_fusion.5.refs_9_), channel_id=1, source_target_pairs={{0,8},{8,0},{16,24},{24,16},{1,9},{9,1},{17,25},{25,17},{2,10},{10... | collective-permute-start | bytes 2752520 | tf_op jit(solution)/shard_map/ppermute | solution.py:231
  240.7 24.4 %collective-permute-start.14 = (bf16[4,2,512,128]{3,2,1,0:T(8,128)(2,1)}, bf16[4,2,512,128]{3,2,1,0:T(8,128)(2,1)S(1)}, u32[]{:S(2)}, u32[]{:S(2)}) collective-permute-start(bf16[4,2,512,128]{3,2,1,0:T(8,128)(2,1)} %get-tuple-element.63.refs_16_), channel_id=1, source_target_pairs={{0,16},{8,24},{16,0},{24,8},{1,17},{9,25},{17,1},{25,9},{2,18},{10... | collective-permute-start | bytes 3145736 | tf_op jit(solution)/shard_map/ppermute | solution.py:311
  241.3 21.3 %collective-permute-start.15 = (bf16[1792,256]{1,0:T(8,128)(2,1)}, bf16[1792,256]{1,0:T(8,128)(2,1)S(1)}, u32[]{:S(2)}, u32[]{:S(2)}) collective-permute-start(bf16[1792,256]{1,0:T(8,128)(2,1)} %pad_maximum_fusion.6.refs_10_), channel_id=1, source_target_pairs={{0,8},{8,0},{16,24},{24,16},{1,9},{9,1},{17,25},{25,17},{2,10},{10... | collective-permute-start | bytes 2752520 | tf_op jit(solution)/shard_map/ppermute | solution.py:231
  268.7 55.8 %reduce-scatter.7.cloned.1.call-start = ((), (), s32[]{:S(2)}) async-start(), calls=%async_computation.6 | async-start | bytes 1310720 | tf_op jit(solution)/shard_map/reduce_scatter | solution.py:320
  268.8 23.5 %collective-permute-start.16 = (bf16[4,2,512,128]{3,2,1,0:T(8,128)(2,1)S(1)}, bf16[4,2,512,128]{3,2,1,0:T(8,128)(2,1)}, u32[]{:S(2)}, u32[]{:S(2)}) collective-permute-start(bf16[4,2,512,128]{3,2,1,0:T(8,128)(2,1)S(1)} %copy-done.19), channel_id=1, source_target_pairs={{0,16},{8,24},{16,0},{24,8},{1,17},{9,25},{17,1},{25,9},{2,18},{10... | collective-permute-start | bytes 3145736 | tf_op jit(solution)/shard_map/ppermute | solution.py:311
  269.5 20.2 %collective-permute-start.17 = (bf16[1792,256]{1,0:T(8,128)(2,1)S(1)}, bf16[1792,256]{1,0:T(8,128)(2,1)S(1)}, u32[]{:S(2)}, u32[]{:S(2)}) collective-permute-start(bf16[1792,256]{1,0:T(8,128)(2,1)S(1)} %copy-done.7), channel_id=1, source_target_pairs={{0,8},{8,0},{16,24},{24,16},{1,9},{9,1},{17,25},{25,17},{2,10},{10... | collective-permute-start | bytes 2752520 | tf_op jit(solution)/shard_map/ppermute | solution.py:231
  296.3 56.2 %reduce-scatter.9.cloned.1.call-start = ((), (), s32[]{:S(2)}) async-start(), calls=%async_computation.7 | async-start | bytes 1310720 | tf_op jit(solution)/shard_map/reduce_scatter | solution.py:320
  296.4 24.8 %collective-permute-start.18 = (bf16[4,2,512,128]{3,2,1,0:T(8,128)(2,1)S(1)}, bf16[4,2,512,128]{3,2,1,0:T(8,128)(2,1)S(1)}, u32[]{:S(2)}, u32[]{:S(2)}) collective-permute-start(bf16[4,2,512,128]{3,2,1,0:T(8,128)(2,1)S(1)} %copy-done.18), channel_id=1, source_target_pairs={{0,16},{8,24},{16,0},{24,8},{1,17},{9,25},{17,1},{25,9},{2,18},{10... | collective-permute-start | bytes 3145736 | tf_op jit(solution)/shard_map/ppermute | solution.py:311
  324.6 56.0 %reduce-scatter.11.cloned.1.call-start = ((), (), s32[]{:S(2)}) async-start(), calls=%async_computation.8 | async-start | bytes 1310720 | tf_op jit(solution)/shard_map/reduce_scatter | solution.py:320
  324.6 25.0 %collective-permute-start.19 = (bf16[4,2,512,128]{3,2,1,0:T(8,128)(2,1)}, bf16[4,2,512,128]{3,2,1,0:T(8,128)(2,1)S(1)}, u32[]{:S(2)}, u32[]{:S(2)}) collective-permute-start(bf16[4,2,512,128]{3,2,1,0:T(8,128)(2,1)} %get-tuple-element.78), channel_id=1, source_target_pairs={{0,16},{8,24},{16,0},{24,8},{1,17},{9,25},{17,1},{25,9},{2,18},{10... | collective-permute-start | bytes 3145736 | tf_op jit(solution)/shard_map/ppermute | solution.py:311
  (25 other events, 297.7 us)
Sparse Core Ops, SparseCore 0:
  23.6 83.5 all-gather.1
  268.9 27.3 reduce-scatter.4
  298.7 25.8 reduce-scatter.6
  326.7 25.7 reduce-scatter.8
  354.7 25.7 reduce-scatter.10

commit v3 on v2

--- a/solution.py
+++ b/solution.py
@@ -27,7 +27,7 @@
     return v / (1.0 + jnp.exp(-v))
 
 
-def hidden_kernel(n, n_start, n_gates, n_after, order, *refs):
+def hidden_kernel(n, n_start, n_gates, n_after, act, order, *refs):
     refs = list(refs)
 
     def take(count):
@@ -88,14 +88,16 @@
                 if k == n - 1:
                     if starts:
                         s = s + starts[m][here, :]
+                    if act:
+                        s = silu(s)
                     if gates:
-                        s = silu(gates[m][here, :]) * s
+                        s = gates[m][here, :] * s
                     outs[m][here, :] = s.astype(outs[m].dtype)
                 else:
                     acc[m][here, :] = s
 
 
-def hidden_pair(features, order, pieces, previous, start=(), gates=(), after=()):
+def hidden_pair(features, order, pieces, previous, start=(), gates=(), after=(), act=False):
     n = len(pieces)
     rows, units = pieces[0].shape
     tokens = features.shape[0]
@@ -107,7 +109,7 @@
     n_more = len(start) + len(gates)
     block = pltpu.VMEM((n, rows, units), jnp.bfloat16)
     return pl.pallas_call(
-        functools.partial(hidden_kernel, n, len(start), len(gates), len(after)),
+        functools.partial(hidden_kernel, n, len(start), len(gates), len(after), act),
         in_specs=[pl.BlockSpec(memory_space=pltpu.SMEM)] + [anywhere] * len(args),
         out_specs=[pl.BlockSpec(memory_space=pltpu.VMEM)] * 2,
         scratch_shapes=[pltpu.VMEM((n, tokens, rows), jnp.bfloat16), block, block]
@@ -235,12 +237,12 @@
         gate_far, up_far = from_x(gate_near), from_x(up_near)
         cols = down_on.shape[1]
         half = cols // 2
-        (down_on, down_prev), _ = lax.optimization_barrier(
-            ((down_on, down_prev), (gate_near[1:], up_near[1:], gate_far[0], up_far[0]))
-        )
         down_mine = lax.dynamic_slice_in_dim(down_on, c * half, half, 1)
         down_give = lax.dynamic_slice_in_dim(down_on, (1 - c) * half, half, 1)
         down_pairs = [down_mine, lax.ppermute(down_give, "mp", along_core)]
+        (down_pairs, down_prev), _ = lax.optimization_barrier(
+            ((down_pairs, down_prev), (gate_near[1:], up_near[1:], gate_far[0], up_far[0]))
+        )
         down_near = []
         for r in range(ny):
             start = lax.rem(y + r, ny) * own_units
@@ -273,7 +275,7 @@
         ]
         down_far = from_x(down_send)
 
-        gates = hidden_pair(features, [*far, first], gate_far, gate_old, start=gate_part)
+        gates = hidden_pair(features, [*far, first], gate_far, gate_old, start=gate_part, act=True)
         inner_o, inner_t = hidden_pair(
             features,
             [*far, first],

time: 393 us -> 384 us (0.977)
  waiting for transfers between devices: 202 us -> 196 us
  transfers between devices with their start and end apart: 25 -> 25, of which waited for: 22 -> 20; matrix products, arithmetic and copies ran while one was open for 8% -> 7% of each run, Pallas kernels for 29% -> 29%
where the time goes in v3:
time: 384 us; the launch traced here: 381 us
  waiting for transfers between devices  196 us (51%)
  Pallas kernels  112 us (29%)
  starting transfers between devices  21.7 us (6%)
  local copies, waits for them, and re-layouts  19.4 us (5%)
  other arithmetic  17.5 us (5%)
  between operations  14.4 us (4%)
    ppermute x8, waiting for transfers between devices, from_x(): return [lax.ppermute(p, 'dp', along_x) for p in pieces]  109 us
    pallas_call x4, Pallas kernels, hidden_pair(): pl.pallas_call(functools.partial(hidden_kernel, n, len(start), len(gates)...  59.8 us
    pallas_call x4, Pallas kernels, down_pair(): pl.pallas_call(functools.partial(down_kernel, n, ny, len(after)), grid_sp...  46.7 us
    ppermute x4, waiting for transfers between devices, products(): lax.ppermute(v, 'dp', along_y(ny - 1 - r))  38.9 us
    reduce_scatter x4, waiting for transfers between devices, over_z(): lax.psum_scatter(total, 'mp', scatter_dimension=0, axis_index_groups=same...  33.4 us
    ppermute x8, starting transfers between devices, from_x(): return [lax.ppermute(p, 'dp', along_x) for p in pieces]  9.47 us
  transfers between devices with their start and end apart: 25, of which 20 were waited for; matrix products, arithmetic and copies ran while one was open for 7% of the time, Pallas kernels for 29%

profile of v3, /device:TPU:0, one launch (start us, length us, event | category | flops | bytes accessed | tf_op | source)
XLA Modules:
  0.0 380.9 jit_solution(4163185531811093625)
XLA Ops:
  7.2 3.0 collective-permute-start
  10.2 3.7 constant_dynamic-slice_fusion.7
  16.2 6.2 %collective-permute-done = bf16[512,512]{1,0:T(8,128)(2,1)S(1)} collective-permute-done((bf16[512,512]{1,0:T(8,128)(2,1)}, bf16[512,512]{1,0:T(8,128)(2,1)S(1)}, u32[]{:S(2)}, u32[]{:S(2)}) %collective-permute-start) | collective-permute-done | bytes 524320 | tf_op jit(solution)/shard_map/ppermute | solution.py:253
  30.1 36.6 %collective-permute-done.1.refs_1_ = bf16[1024,896]{1,0:T(8,128)(2,1)} collective-permute-done((bf16[1024,896]{1,0:T(8,128)(2,1)S(1)}, bf16[1024,896]{1,0:T(8,128)(2,1)}, u32[]{:S(2)}, u32[]{:S(2)}) %collective-permute-start.1) | collective-permute-done | bytes 1835040 | tf_op jit(solution)/shard_map/ppermute | solution.py:233
  68.9 35.3 %collective-permute-done.4.refs_1_ = bf16[1024,896]{1,0:T(8,128)(2,1)} collective-permute-done((bf16[1024,896]{1,0:T(8,128)(2,1)}, bf16[1024,896]{1,0:T(8,128)(2,1)}, u32[]{:S(2)}, u32[]{:S(2)}) %collective-permute-start.4) | collective-permute-done | bytes 1835040 | tf_op jit(solution)/shard_map/ppermute | solution.py:233
  112.5 5.6 %shard_map.90 = bf16[896,2048]{1,0:T(8,128)(2,1)} custom-call(s32[2]{0:T(128)} %pad_add_fusion.at, bf16[1792,4096]{1,0:T(8,128)(2,1)} %refs_11_.3), custom_call_target="tpu_custom_call" | custom-call | flops 1 | bytes 1 | tf_op jit(solution)/shard_map/pallas_call | solution.py:189
  120.2 14.4 %shard_map.87 = (f32[1024,896]{1,0:T(8,128)}, f32[1024,896]{1,0:T(8,128)}) custom-call(s32[3]{0:T(128)} %add_add_fusion.1.order, bf16[1024,4096]{1,0:T(8,128)(2,1)} %all-gather.2.cloned.1.call-done.refs_0_, bf16[1024,896]{1,0:T(8,128)(2,1)} %get-tuple-element.91.refs_1_, bf16[1024,896]{1,0:T(8,128)(2,1)} %collective-permute-done.5.refs_2_, ...), custom_call_target="tpu_custom_call" | custom-call | flops 1 | bytes 1 | tf_op jit(solution)/shard_map/pallas_call | solution.py:111
  134.6 14.5 %shard_map.86 = (f32[1024,896]{1,0:T(8,128)}, f32[1024,896]{1,0:T(8,128)}) custom-call(s32[3]{0:T(128)} %add_add_fusion.1.order, bf16[1024,4096]{1,0:T(8,128)(2,1)} %all-gather.2.cloned.1.call-done.refs_0_, bf16[1024,896]{1,0:T(8,128)(2,1)} %copy-done.2, bf16[1024,896]{1,0:T(8,128)(2,1)} %collective-permute-done.2.refs_2_, bf16[4096,1792]{1,0:T(8,128)(2,1)} %refs_3_.7), custom_call_target="tpu_custom_call" | custom-call | flops 1 | bytes 1 | tf_op jit(solution)/shard_map/pallas_call | solution.py:111
  155.3 15.8 %shard_map.88 = (f32[1024,896]{1,0:T(8,128)}, f32[1024,896]{1,0:T(8,128)}) custom-call(s32[3]{0:T(128)} %add_add_fusion.order, bf16[1024,4096]{1,0:T(8,128)(2,1)} %all-gather.2.cloned.1.call-done.refs_0_, bf16[1024,896]{1,0:T(8,128)(2,1)} %collective-permute-done.4.refs_1_, bf16[1024,896]{1,0:T(8,128)(2,1)} %collective-permute-done.6.refs_2_, ...), custom_call_target="tpu_custom_call" | custom-call | flops 1 | bytes 1 | tf_op jit(solution)/shard_map/pallas_call | solution.py:111
  174.6 18.4 %collective-permute-done.3.refs_2_ = bf16[1024,896]{1,0:T(8,128)(2,1)} collective-permute-done((bf16[1024,896]{1,0:T(8,128)(2,1)}, bf16[1024,896]{1,0:T(8,128)(2,1)}, u32[]{:S(2)}, u32[]{:S(2)}) %collective-permute-start.3) | collective-permute-done | bytes 1835040 | tf_op jit(solution)/shard_map/ppermute | solution.py:233
  193.0 15.1 %shard_map.89 = (bf16[1024,896]{1,0:T(8,128)(2,1)}, bf16[1024,896]{1,0:T(8,128)(2,1)}) custom-call(s32[3]{0:T(128)} %add_add_fusion.order, bf16[1024,4096]{1,0:T(8,128)(2,1)} %all-gather.2.cloned.1.call-done.refs_0_, bf16[1024,896]{1,0:T(8,128)(2,1)} %collective-permute-done.1.refs_1_, bf16[1024,896]{1,0:T(8,128)(2,1)} %collective-permute-done.3.refs_2_, ...), custom_call_target="tpu_custom_call" | custom-call | flops 1 | bytes 1 | tf_op jit(solution)/shard_map/pallas_call | solution.py:111
  211.4 3.9 %collective-permute-done.10.refs_1_ = bf16[1024,896]{1,0:T(8,128)(2,1)S(1)} collective-permute-done((bf16[1024,896]{1,0:T(8,128)(2,1)}, bf16[1024,896]{1,0:T(8,128)(2,1)S(1)}, u32[]{:S(2)}, u32[]{:S(2)}) %collective-permute-start.10) | collective-permute-done | bytes 1835040 | tf_op jit(solution)/shard_map/ppermute | solution.py:294
  216.6 11.4 %shard_map.91 = (bf16[4,2,512,128]{3,2,1,0:T(8,128)(2,1)}, f32[4,2,512,128]{3,2,1,0:T(8,128)}) custom-call(s32[17]{0:T(128)} %stack.180.at, bf16[1024,896]{1,0:T(8,128)(2,1)} %get-tuple-element.59.refs_0_, bf16[1024,896]{1,0:T(8,128)(2,1)} %copy-done.1, bf16[1024,896]{1,0:T(8,128)(2,1)} %get-tuple-element.60.refs_2_, ...), custom_call_target="tpu_custom_call" | custom-call | flops 1 | bytes 1 | tf_op jit(solution)/shard_map/pallas_call | solution.py:153
  228.1 3.8 collective-permute-done.13.refs_6_.refs_7_
  234.5 11.9 %shard_map.92 = (bf16[4,2,512,128]{3,2,1,0:T(8,128)(2,1)}, f32[4,2,512,128]{3,2,1,0:T(8,128)}) custom-call(s32[17]{0:T(128)} %stack.194.at, bf16[1024,896]{1,0:T(8,128)(2,1)} %get-tuple-element.59.refs_0_, bf16[1024,896]{1,0:T(8,128)(2,1)} %copy-done.1, bf16[1024,896]{1,0:T(8,128)(2,1)} %get-tuple-element.60.refs_2_, ...), custom_call_target="tpu_custom_call" | custom-call | flops 1 | bytes 1 | tf_op jit(solution)/shard_map/pallas_call | solution.py:153
  246.3 7.7 %collective-permute-done.15.refs_6_.refs_7_ = bf16[1792,256]{1,0:T(8,128)(2,1)S(1)} collective-permute-done((bf16[1792,256]{1,0:T(8,128)(2,1)}, bf16[1792,256]{1,0:T(8,128)(2,1)S(1)}, u32[]{:S(2)}, u32[]{:S(2)}) %collective-permute-start.15) | collective-permute-done | bytes 917536 | tf_op jit(solution)/shard_map/ppermute | solution.py:233
  257.3 2.5 add_convert_fusion.3.refs_17_
  262.7 11.8 %shard_map.93 = (bf16[4,2,512,128]{3,2,1,0:T(8,128)(2,1)}, f32[4,2,512,128]{3,2,1,0:T(8,128)}) custom-call(s32[17]{0:T(128)} %stack.203.at, bf16[1024,896]{1,0:T(8,128)(2,1)} %get-tuple-element.59.refs_0_, bf16[1024,896]{1,0:T(8,128)(2,1)} %copy-done.1, bf16[1024,896]{1,0:T(8,128)(2,1)} %get-tuple-element.60.refs_2_, ...), custom_call_target="tpu_custom_call" | custom-call | flops 1 | bytes 1 | tf_op jit(solution)/shard_map/pallas_call | solution.py:153
  274.5 6.6 %collective-permute-done.17.refs_6_.refs_7_ = bf16[1792,256]{1,0:T(8,128)(2,1)S(1)} collective-permute-done((bf16[1792,256]{1,0:T(8,128)(2,1)S(1)}, bf16[1792,256]{1,0:T(8,128)(2,1)S(1)}, u32[]{:S(2)}, u32[]{:S(2)}) %collective-permute-start.17) | collective-permute-done | bytes 917536 | tf_op jit(solution)/shard_map/ppermute | solution.py:233
  283.4 2.5 add_convert_fusion.2.refs_17_
  289.7 11.7 %shard_map.94 = (bf16[4,2,512,128]{3,2,1,0:T(8,128)(2,1)}, f32[4,2,512,128]{3,2,1,0:T(8,128)}) custom-call(s32[17]{0:T(128)} %stack.212.at, bf16[1024,896]{1,0:T(8,128)(2,1)} %get-tuple-element.59.refs_0_, bf16[1024,896]{1,0:T(8,128)(2,1)} %copy-done.1, bf16[1024,896]{1,0:T(8,128)(2,1)} %get-tuple-element.60.refs_2_, ...), custom_call_target="tpu_custom_call" | custom-call | flops 1 | bytes 1 | tf_op jit(solution)/shard_map/pallas_call | solution.py:153
  301.4 11.0 %collective-permute-done.18 = bf16[4,2,512,128]{3,2,1,0:T(8,128)(2,1)S(1)} collective-permute-done((bf16[4,2,512,128]{3,2,1,0:T(8,128)(2,1)S(1)}, bf16[4,2,512,128]{3,2,1,0:T(8,128)(2,1)S(1)}, u32[]{:S(2)}, u32[]{:S(2)}) %collective-permute-start.18) | collective-permute-done | bytes 1048608 | tf_op jit(solution)/shard_map/ppermute | solution.py:313
  317.3 23.5 %collective-permute-done.19 = bf16[4,2,512,128]{3,2,1,0:T(8,128)(2,1)S(1)} collective-permute-done((bf16[4,2,512,128]{3,2,1,0:T(8,128)(2,1)}, bf16[4,2,512,128]{3,2,1,0:T(8,128)(2,1)S(1)}, u32[]{:S(2)}, u32[]{:S(2)}) %collective-permute-start.19) | collective-permute-done | bytes 1048608 | tf_op jit(solution)/shard_map/ppermute | solution.py:313
  343.7 28.1 %reduce-scatter.11.cloned.1.call-done = bf16[1,2,512,128]{3,2,1,0:T(8,128)(2,1)} async-done(((bf16[4,2,512,128]{3,2,1,0:T(8,128)(2,1)}), bf16[1,2,512,128]{3,2,1,0:T(8,128)(2,1)}) %reduce-scatter.11.cloned.1.call-update) | async-done | bytes 262160 | tf_op jit(solution)/shard_map/reduce_scatter | solution.py:322
  (116 shorter events, 61.3 us)
Async XLA Ops:
  7.2 113.0 %all-gather.2.cloned.1.call-start = ((), (), s32[]{:S(2)}) async-start(), calls=%async_computation.4 | async-start | bytes 9437184 | tf_op jit(solution)/shard_map/all_gather | solution.py:255
  7.2 15.2 %collective-permute-start = (bf16[512,512]{1,0:T(8,128)(2,1)}, bf16[512,512]{1,0:T(8,128)(2,1)S(1)}, u32[]{:S(2)}, u32[]{:S(2)}) collective-permute-start(bf16[512,512]{1,0:T(8,128)(2,1)} %param.7), channel_id=1, source_target_pairs={{0,16},{8,24},{16,0},{24,8},{1,17},{9,25},{17,1},{25,9},{2,18},{10... | collective-permute-start | bytes 1572872 | tf_op jit(solution)/shard_map/ppermute | solution.py:253
  23.5 264.0 %reduce-scatter.5.cloned.1.call-start = ((), (), s32[]{:S(2)}) async-start(), calls=%async_computation.5 | async-start | bytes 1310720 | tf_op jit(solution)/shard_map/reduce_scatter | solution.py:322
  23.5 43.2 %collective-permute-start.1 = (bf16[1024,896]{1,0:T(8,128)(2,1)S(1)}, bf16[1024,896]{1,0:T(8,128)(2,1)}, u32[]{:S(2)}, u32[]{:S(2)}) collective-permute-start(bf16[1024,896]{1,0:T(8,128)(2,1)S(1)} %get-tuple-element.93.refs_1_), channel_id=1, source_target_pairs={{0,8},{8,0},{16,24},{24,16},{1,9},{9,1},{17,25},{25,17},{2,10},{10... | collective-permute-start | bytes 5505032 | tf_op jit(solution)/shard_map/ppermute | solution.py:233
  25.3 78.9 %collective-permute-start.4 = (bf16[1024,896]{1,0:T(8,128)(2,1)}, bf16[1024,896]{1,0:T(8,128)(2,1)}, u32[]{:S(2)}, u32[]{:S(2)}) collective-permute-start(bf16[1024,896]{1,0:T(8,128)(2,1)} %get-tuple-element.91.refs_1_), channel_id=1, source_target_pairs={{0,8},{8,0},{16,24},{24,16},{1,9},{9,1},{17,25},{25,17},{2,10},{10... | collective-permute-start | bytes 5505032 | tf_op jit(solution)/shard_map/ppermute | solution.py:233
  25.7 43.3 %collective-permute-start.2 = (bf16[1024,896]{1,0:T(8,128)(2,1)}, bf16[1024,896]{1,0:T(8,128)(2,1)}, u32[]{:S(2)}, u32[]{:S(2)}) collective-permute-start(bf16[1024,896]{1,0:T(8,128)(2,1)} %get-tuple-element.92), channel_id=1, source_target_pairs={{0,16},{8,24},{16,0},{24,8},{1,17},{9,25},{17,1},{25,9},{2,18},{10... | collective-permute-start | bytes 5505032 | tf_op jit(solution)/shard_map/ppermute | solution.py:229
  27.4 78.5 %collective-permute-start.5 = (bf16[1024,896]{1,0:T(8,128)(2,1)}, bf16[1024,896]{1,0:T(8,128)(2,1)}, u32[]{:S(2)}, u32[]{:S(2)}) collective-permute-start(bf16[1024,896]{1,0:T(8,128)(2,1)} %get-tuple-element.90), channel_id=1, source_target_pairs={{0,16},{8,24},{16,0},{24,8},{1,17},{9,25},{17,1},{25,9},{2,18},{10... | collective-permute-start | bytes 5505032 | tf_op jit(solution)/shard_map/ppermute | solution.py:229
  30.0 75.9 %collective-permute-start.7 = (bf16[1792,512]{1,0:T(8,128)(2,1)S(1)}, bf16[1792,512]{1,0:T(8,128)(2,1)S(1)}, u32[]{:S(2)}, u32[]{:S(2)}) collective-permute-start(bf16[1792,512]{1,0:T(8,128)(2,1)S(1)} %get-tuple-element.88), channel_id=1, source_target_pairs={{0,1},{1,0},{2,3},{3,2},{4,5},{5,4},{6,7},{7,6},{8,9},{9,8},{10,11... | collective-permute-start | bytes 5505032 | tf_op jit(solution)/shard_map/ppermute | solution.py:242
  108.4 40.7 %collective-permute-start.8 = (bf16[1792,512]{1,0:T(8,128)(2,1)}, bf16[1792,512]{1,0:T(8,128)(2,1)}, u32[]{:S(2)}, u32[]{:S(2)}) collective-permute-start(bf16[1792,512]{1,0:T(8,128)(2,1)} %pad_maximum_fusion.1), channel_id=1, source_target_pairs={{0,16},{8,24},{16,0},{24,8},{1,17},{9,25},{17,1},{25,9},{2,18},{10... | collective-permute-start | bytes 5505032 | tf_op jit(solution)/shard_map/ppermute | solution.py:252
  110.5 44.8 %collective-permute-start.6 = (bf16[1024,896]{1,0:T(8,128)(2,1)}, bf16[1024,896]{1,0:T(8,128)(2,1)}, u32[]{:S(2)}, u32[]{:S(2)}) collective-permute-start(bf16[1024,896]{1,0:T(8,128)(2,1)} %collective-permute-done.5.refs_2_), channel_id=1, source_target_pairs={{0,8},{8,0},{16,24},{24,16},{1,9},{9,1},{17,25},{25,17},{2,10},{10... | collective-permute-start | bytes 5505032 | tf_op jit(solution)/shard_map/ppermute | solution.py:233
  118.1 93.3 %collective-permute-start.12 = (bf16[896,2048]{1,0:T(8,128)(2,1)}, bf16[896,2048]{1,0:T(8,128)(2,1)}, u32[]{:S(2)}, u32[]{:S(2)}) collective-permute-start(bf16[896,2048]{1,0:T(8,128)(2,1)} %shard_map.90), channel_id=1, source_target_pairs={{0,1},{1,0},{2,3},{3,2},{4,5},{5,4},{6,7},{7,6},{8,9},{9,8},{10,11... | collective-permute-start | bytes 11010056 | tf_op jit(solution)/shard_map/ppermute | solution.py:264
  118.2 74.8 %collective-permute-start.3 = (bf16[1024,896]{1,0:T(8,128)(2,1)}, bf16[1024,896]{1,0:T(8,128)(2,1)}, u32[]{:S(2)}, u32[]{:S(2)}) collective-permute-start(bf16[1024,896]{1,0:T(8,128)(2,1)} %collective-permute-done.2.refs_2_), channel_id=1, source_target_pairs={{0,8},{8,0},{16,24},{24,16},{1,9},{9,1},{17,25},{25,17},{2,10},{10... | collective-permute-start | bytes 5505032 | tf_op jit(solution)/shard_map/ppermute | solution.py:233
  153.1 55.7 %collective-permute-start.9 = (bf16[1792,256]{1,0:T(8,128)(2,1)S(1)}, bf16[1792,256]{1,0:T(8,128)(2,1)S(1)}, u32[]{:S(2)}, u32[]{:S(2)}) collective-permute-start(bf16[1792,256]{1,0:T(8,128)(2,1)S(1)} %pad_maximum_fusion.4.refs_8_), channel_id=1, source_target_pairs={{0,8},{8,0},{16,24},{24,16},{1,9},{9,1},{17,25},{25,17},{2,10},{10... | collective-permute-start | bytes 2752520 | tf_op jit(solution)/shard_map/ppermute | solution.py:233
  208.8 6.7 %collective-permute-start.11 = (bf16[1024,896]{1,0:T(8,128)(2,1)}, bf16[1024,896]{1,0:T(8,128)(2,1)}, u32[]{:S(2)}, u32[]{:S(2)}) collective-permute-start(bf16[1024,896]{1,0:T(8,128)(2,1)} %get-tuple-element.60.refs_2_), channel_id=1, source_target_pairs={{0,1},{1,0},{2,3},{3,2},{4,5},{5,4},{6,7},{7,6},{8,9},{9,8},{10,11... | collective-permute-start | bytes 5505032 | tf_op jit(solution)/shard_map/ppermute | solution.py:294
  209.3 22.6 %collective-permute-start.13 = (bf16[1792,256]{1,0:T(8,128)(2,1)}, bf16[1792,256]{1,0:T(8,128)(2,1)}, u32[]{:S(2)}, u32[]{:S(2)}) collective-permute-start(bf16[1792,256]{1,0:T(8,128)(2,1)} %pad_maximum_fusion.5.refs_9_), channel_id=1, source_target_pairs={{0,8},{8,0},{16,24},{24,16},{1,9},{9,1},{17,25},{25,17},{2,10},{10... | collective-permute-start | bytes 2752520 | tf_op jit(solution)/shard_map/ppermute | solution.py:233
  231.9 24.4 %collective-permute-start.14 = (bf16[4,2,512,128]{3,2,1,0:T(8,128)(2,1)}, bf16[4,2,512,128]{3,2,1,0:T(8,128)(2,1)S(1)}, u32[]{:S(2)}, u32[]{:S(2)}) collective-permute-start(bf16[4,2,512,128]{3,2,1,0:T(8,128)(2,1)} %get-tuple-element.65.refs_16_), channel_id=1, source_target_pairs={{0,16},{8,24},{16,0},{24,8},{1,17},{9,25},{17,1},{25,9},{2,18},{10... | collective-permute-start | bytes 3145736 | tf_op jit(solution)/shard_map/ppermute | solution.py:313
  232.7 21.3 %collective-permute-start.15 = (bf16[1792,256]{1,0:T(8,128)(2,1)}, bf16[1792,256]{1,0:T(8,128)(2,1)S(1)}, u32[]{:S(2)}, u32[]{:S(2)}) collective-permute-start(bf16[1792,256]{1,0:T(8,128)(2,1)} %pad_maximum_fusion.6.refs_10_), channel_id=1, source_target_pairs={{0,8},{8,0},{16,24},{24,16},{1,9},{9,1},{17,25},{25,17},{2,10},{10... | collective-permute-start | bytes 2752520 | tf_op jit(solution)/shard_map/ppermute | solution.py:233
  259.9 55.8 %reduce-scatter.7.cloned.1.call-start = ((), (), s32[]{:S(2)}) async-start(), calls=%async_computation.6 | async-start | bytes 1310720 | tf_op jit(solution)/shard_map/reduce_scatter | solution.py:322
  259.9 23.5 %collective-permute-start.16 = (bf16[4,2,512,128]{3,2,1,0:T(8,128)(2,1)S(1)}, bf16[4,2,512,128]{3,2,1,0:T(8,128)(2,1)}, u32[]{:S(2)}, u32[]{:S(2)}) collective-permute-start(bf16[4,2,512,128]{3,2,1,0:T(8,128)(2,1)S(1)} %copy-done.18), channel_id=1, source_target_pairs={{0,16},{8,24},{16,0},{24,8},{1,17},{9,25},{17,1},{25,9},{2,18},{10... | collective-permute-start | bytes 3145736 | tf_op jit(solution)/shard_map/ppermute | solution.py:313
  260.9 20.2 %collective-permute-start.17 = (bf16[1792,256]{1,0:T(8,128)(2,1)S(1)}, bf16[1792,256]{1,0:T(8,128)(2,1)S(1)}, u32[]{:S(2)}, u32[]{:S(2)}) collective-permute-start(bf16[1792,256]{1,0:T(8,128)(2,1)S(1)} %copy-done.7), channel_id=1, source_target_pairs={{0,8},{8,0},{16,24},{24,16},{1,9},{9,1},{17,25},{25,17},{2,10},{10... | collective-permute-start | bytes 2752520 | tf_op jit(solution)/shard_map/ppermute | solution.py:233
  287.5 56.2 %reduce-scatter.9.cloned.1.call-start = ((), (), s32[]{:S(2)}) async-start(), calls=%async_computation.7 | async-start | bytes 1310720 | tf_op jit(solution)/shard_map/reduce_scatter | solution.py:322
  287.6 24.8 %collective-permute-start.18 = (bf16[4,2,512,128]{3,2,1,0:T(8,128)(2,1)S(1)}, bf16[4,2,512,128]{3,2,1,0:T(8,128)(2,1)S(1)}, u32[]{:S(2)}, u32[]{:S(2)}) collective-permute-start(bf16[4,2,512,128]{3,2,1,0:T(8,128)(2,1)S(1)} %copy-done.17), channel_id=1, source_target_pairs={{0,16},{8,24},{16,0},{24,8},{1,17},{9,25},{17,1},{25,9},{2,18},{10... | collective-permute-start | bytes 3145736 | tf_op jit(solution)/shard_map/ppermute | solution.py:313
  315.7 56.0 %reduce-scatter.11.cloned.1.call-start = ((), (), s32[]{:S(2)}) async-start(), calls=%async_computation.8 | async-start | bytes 1310720 | tf_op jit(solution)/shard_map/reduce_scatter | solution.py:322
  315.8 25.0 %collective-permute-start.19 = (bf16[4,2,512,128]{3,2,1,0:T(8,128)(2,1)}, bf16[4,2,512,128]{3,2,1,0:T(8,128)(2,1)S(1)}, u32[]{:S(2)}, u32[]{:S(2)}) collective-permute-start(bf16[4,2,512,128]{3,2,1,0:T(8,128)(2,1)} %get-tuple-element.80), channel_id=1, source_target_pairs={{0,16},{8,24},{16,0},{24,8},{1,17},{9,25},{17,1},{25,9},{2,18},{10... | collective-permute-start | bytes 3145736 | tf_op jit(solution)/shard_map/ppermute | solution.py:313
  (24 other events, 296.0 us)
Sparse Core Ops, SparseCore 0:
  23.6 83.5 all-gather.1
  260.0 27.4 reduce-scatter.4
  289.9 25.7 reduce-scatter.6
  317.9 25.7 reduce-scatter.8
  345.9 25.8 reduce-scatter.10

commit v4 on v3

--- a/solution.py
+++ b/solution.py
@@ -240,9 +240,10 @@
         down_mine = lax.dynamic_slice_in_dim(down_on, c * half, half, 1)
         down_give = lax.dynamic_slice_in_dim(down_on, (1 - c) * half, half, 1)
         down_pairs = [down_mine, lax.ppermute(down_give, "mp", along_core)]
-        (down_pairs, down_prev), _ = lax.optimization_barrier(
-            ((down_pairs, down_prev), (gate_near[1:], up_near[1:], gate_far[0], up_far[0]))
+        down_pairs, _ = lax.optimization_barrier(
+            (down_pairs, (gate_near[1:], up_near[1:], gate_far[0], up_far[0]))
         )
+        down_prev, _ = lax.optimization_barrier((down_prev, (gate_near[1:], gate_far[0])))
         down_near = []
         for r in range(ny):
             start = lax.rem(y + r, ny) * own_units

time: 384 us -> 384 us (level)
  no operation moved by 1% of the time
where the time goes in v4:
time: 384 us; the launch traced here: 381 us
  waiting for transfers between devices  196 us (51%)
  Pallas kernels  112 us (29%)
  starting transfers between devices  21.8 us (6%)
  local copies, waits for them, and re-layouts  19.4 us (5%)
  other arithmetic  17.4 us (5%)
  between operations  14.4 us (4%)
    ppermute x8, waiting for transfers between devices, from_x(): return [lax.ppermute(p, 'dp', along_x) for p in pieces]  110 us
    pallas_call x4, Pallas kernels, hidden_pair(): pl.pallas_call(functools.partial(hidden_kernel, n, len(start), len(gates)...  59.8 us
    pallas_call x4, Pallas kernels, down_pair(): pl.pallas_call(functools.partial(down_kernel, n, ny, len(after)), grid_sp...  46.8 us
    ppermute x4, waiting for transfers between devices, products(): lax.ppermute(v, 'dp', along_y(ny - 1 - r))  38.8 us
    reduce_scatter x4, waiting for transfers between devices, over_z(): lax.psum_scatter(total, 'mp', scatter_dimension=0, axis_index_groups=same...  33.3 us
    ppermute x8, starting transfers between devices, from_x(): return [lax.ppermute(p, 'dp', along_x) for p in pieces]  9.5 us
  transfers between devices with their start and end apart: 25, of which 20 were waited for; matrix products, arithmetic and copies ran while one was open for 7% of the time, Pallas kernels for 29%

profile of v4, /device:TPU:0, one launch (start us, length us, event | category | flops | bytes accessed | tf_op | source)
XLA Modules:
  0.0 380.9 jit_solution(13932481552524793547)
XLA Ops:
  7.2 3.0 collective-permute-start
  10.2 3.7 constant_dynamic-slice_fusion.6
  16.1 6.2 %collective-permute-done = bf16[512,512]{1,0:T(8,128)(2,1)S(1)} collective-permute-done((bf16[512,512]{1,0:T(8,128)(2,1)}, bf16[512,512]{1,0:T(8,128)(2,1)S(1)}, u32[]{:S(2)}, u32[]{:S(2)}) %collective-permute-start) | collective-permute-done | bytes 524320 | tf_op jit(solution)/shard_map/ppermute | solution.py:254
  30.0 36.8 %collective-permute-done.1.refs_1_ = bf16[1024,896]{1,0:T(8,128)(2,1)} collective-permute-done((bf16[1024,896]{1,0:T(8,128)(2,1)}, bf16[1024,896]{1,0:T(8,128)(2,1)}, u32[]{:S(2)}, u32[]{:S(2)}) %collective-permute-start.1) | collective-permute-done | bytes 1835040 | tf_op jit(solution)/shard_map/ppermute | solution.py:233
  68.9 35.5 %collective-permute-done.4.refs_1_ = bf16[1024,896]{1,0:T(8,128)(2,1)} collective-permute-done((bf16[1024,896]{1,0:T(8,128)(2,1)S(1)}, bf16[1024,896]{1,0:T(8,128)(2,1)}, u32[]{:S(2)}, u32[]{:S(2)}) %collective-permute-start.4) | collective-permute-done | bytes 1835040 | tf_op jit(solution)/shard_map/ppermute | solution.py:233
  112.5 5.6 %shard_map.90 = bf16[896,2048]{1,0:T(8,128)(2,1)} custom-call(s32[2]{0:T(128)} %pad_add_fusion.at, bf16[1792,4096]{1,0:T(8,128)(2,1)} %refs_11_.3), custom_call_target="tpu_custom_call" | custom-call | flops 1 | bytes 1 | tf_op jit(solution)/shard_map/pallas_call | solution.py:189
  120.2 14.3 %shard_map.86 = (f32[1024,896]{1,0:T(8,128)}, f32[1024,896]{1,0:T(8,128)}) custom-call(s32[3]{0:T(128)} %add_add_fusion.1.order, bf16[1024,4096]{1,0:T(8,128)(2,1)} %all-gather.2.cloned.1.call-done.refs_0_, bf16[1024,896]{1,0:T(8,128)(2,1)} %get-tuple-element.93.refs_1_, bf16[1024,896]{1,0:T(8,128)(2,1)} %collective-permute-done.2.refs_2_, ...), custom_call_target="tpu_custom_call" | custom-call | flops 1 | bytes 1 | tf_op jit(solution)/shard_map/pallas_call | solution.py:111
  134.5 14.6 %shard_map.87 = (f32[1024,896]{1,0:T(8,128)}, f32[1024,896]{1,0:T(8,128)}) custom-call(s32[3]{0:T(128)} %add_add_fusion.1.order, bf16[1024,4096]{1,0:T(8,128)(2,1)} %all-gather.2.cloned.1.call-done.refs_0_, bf16[1024,896]{1,0:T(8,128)(2,1)} %copy-done.2, bf16[1024,896]{1,0:T(8,128)(2,1)} %collective-permute-done.5.refs_2_, bf16[4096,1792]{1,0:T(8,128)(2,1)} %refs_3_.6), custom_call_target="tpu_custom_call" | custom-call | flops 1 | bytes 1 | tf_op jit(solution)/shard_map/pallas_call | solution.py:111
  149.1 2.5 fusion.1
  155.2 15.8 %shard_map.88 = (f32[1024,896]{1,0:T(8,128)}, f32[1024,896]{1,0:T(8,128)}) custom-call(s32[3]{0:T(128)} %add_add_fusion.order, bf16[1024,4096]{1,0:T(8,128)(2,1)} %all-gather.2.cloned.1.call-done.refs_0_, bf16[1024,896]{1,0:T(8,128)(2,1)} %collective-permute-done.4.refs_1_, bf16[1024,896]{1,0:T(8,128)(2,1)} %collective-permute-done.6.refs_2_, ...), custom_call_target="tpu_custom_call" | custom-call | flops 1 | bytes 1 | tf_op jit(solution)/shard_map/pallas_call | solution.py:111
  174.5 18.6 %collective-permute-done.3.refs_2_ = bf16[1024,896]{1,0:T(8,128)(2,1)} collective-permute-done((bf16[1024,896]{1,0:T(8,128)(2,1)}, bf16[1024,896]{1,0:T(8,128)(2,1)}, u32[]{:S(2)}, u32[]{:S(2)}) %collective-permute-start.3) | collective-permute-done | bytes 1835040 | tf_op jit(solution)/shard_map/ppermute | solution.py:233
  193.0 15.1 %shard_map.89 = (bf16[1024,896]{1,0:T(8,128)(2,1)}, bf16[1024,896]{1,0:T(8,128)(2,1)}) custom-call(s32[3]{0:T(128)} %add_add_fusion.order, bf16[1024,4096]{1,0:T(8,128)(2,1)} %all-gather.2.cloned.1.call-done.refs_0_, bf16[1024,896]{1,0:T(8,128)(2,1)} %collective-permute-done.1.refs_1_, bf16[1024,896]{1,0:T(8,128)(2,1)} %collective-permute-done.3.refs_2_, ...), custom_call_target="tpu_custom_call" | custom-call | flops 1 | bytes 1 | tf_op jit(solution)/shard_map/pallas_call | solution.py:111
  211.4 3.9 %collective-permute-done.10.refs_1_ = bf16[1024,896]{1,0:T(8,128)(2,1)S(1)} collective-permute-done((bf16[1024,896]{1,0:T(8,128)(2,1)}, bf16[1024,896]{1,0:T(8,128)(2,1)S(1)}, u32[]{:S(2)}, u32[]{:S(2)}) %collective-permute-start.10) | collective-permute-done | bytes 1835040 | tf_op jit(solution)/shard_map/ppermute | solution.py:295
  216.6 11.4 %shard_map.91 = (bf16[4,2,512,128]{3,2,1,0:T(8,128)(2,1)}, f32[4,2,512,128]{3,2,1,0:T(8,128)}) custom-call(s32[17]{0:T(128)} %stack.180.at, bf16[1024,896]{1,0:T(8,128)(2,1)} %get-tuple-element.59.refs_0_, bf16[1024,896]{1,0:T(8,128)(2,1)} %copy-done.1, bf16[1024,896]{1,0:T(8,128)(2,1)} %get-tuple-element.60.refs_2_, ...), custom_call_target="tpu_custom_call" | custom-call | flops 1 | bytes 1 | tf_op jit(solution)/shard_map/pallas_call | solution.py:153
  228.1 3.8 collective-permute-done.13.refs_6_.refs_7_
  234.6 11.9 %shard_map.92 = (bf16[4,2,512,128]{3,2,1,0:T(8,128)(2,1)}, f32[4,2,512,128]{3,2,1,0:T(8,128)}) custom-call(s32[17]{0:T(128)} %stack.194.at, bf16[1024,896]{1,0:T(8,128)(2,1)} %get-tuple-element.59.refs_0_, bf16[1024,896]{1,0:T(8,128)(2,1)} %copy-done.1, bf16[1024,896]{1,0:T(8,128)(2,1)} %get-tuple-element.60.refs_2_, ...), custom_call_target="tpu_custom_call" | custom-call | flops 1 | bytes 1 | tf_op jit(solution)/shard_map/pallas_call | solution.py:153
  246.5 7.6 %collective-permute-done.15.refs_6_.refs_7_ = bf16[1792,256]{1,0:T(8,128)(2,1)S(1)} collective-permute-done((bf16[1792,256]{1,0:T(8,128)(2,1)}, bf16[1792,256]{1,0:T(8,128)(2,1)S(1)}, u32[]{:S(2)}, u32[]{:S(2)}) %collective-permute-start.15) | collective-permute-done | bytes 917536 | tf_op jit(solution)/shard_map/ppermute | solution.py:233
  257.3 2.5 add_convert_fusion.3.refs_17_
  262.7 11.8 %shard_map.93 = (bf16[4,2,512,128]{3,2,1,0:T(8,128)(2,1)}, f32[4,2,512,128]{3,2,1,0:T(8,128)}) custom-call(s32[17]{0:T(128)} %stack.203.at, bf16[1024,896]{1,0:T(8,128)(2,1)} %get-tuple-element.59.refs_0_, bf16[1024,896]{1,0:T(8,128)(2,1)} %copy-done.1, bf16[1024,896]{1,0:T(8,128)(2,1)} %get-tuple-element.60.refs_2_, ...), custom_call_target="tpu_custom_call" | custom-call | flops 1 | bytes 1 | tf_op jit(solution)/shard_map/pallas_call | solution.py:153
  274.5 6.6 %collective-permute-done.17.refs_6_.refs_7_ = bf16[1792,256]{1,0:T(8,128)(2,1)S(1)} collective-permute-done((bf16[1792,256]{1,0:T(8,128)(2,1)S(1)}, bf16[1792,256]{1,0:T(8,128)(2,1)S(1)}, u32[]{:S(2)}, u32[]{:S(2)}) %collective-permute-start.17) | collective-permute-done | bytes 917536 | tf_op jit(solution)/shard_map/ppermute | solution.py:233
  289.8 11.7 %shard_map.94 = (bf16[4,2,512,128]{3,2,1,0:T(8,128)(2,1)}, f32[4,2,512,128]{3,2,1,0:T(8,128)}) custom-call(s32[17]{0:T(128)} %stack.212.at, bf16[1024,896]{1,0:T(8,128)(2,1)} %get-tuple-element.59.refs_0_, bf16[1024,896]{1,0:T(8,128)(2,1)} %copy-done.1, bf16[1024,896]{1,0:T(8,128)(2,1)} %get-tuple-element.60.refs_2_, ...), custom_call_target="tpu_custom_call" | custom-call | flops 1 | bytes 1 | tf_op jit(solution)/shard_map/pallas_call | solution.py:153
  301.5 10.9 %collective-permute-done.18 = bf16[4,2,512,128]{3,2,1,0:T(8,128)(2,1)S(1)} collective-permute-done((bf16[4,2,512,128]{3,2,1,0:T(8,128)(2,1)S(1)}, bf16[4,2,512,128]{3,2,1,0:T(8,128)(2,1)S(1)}, u32[]{:S(2)}, u32[]{:S(2)}) %collective-permute-start.18) | collective-permute-done | bytes 1048608 | tf_op jit(solution)/shard_map/ppermute | solution.py:314
  317.3 23.5 %collective-permute-done.19 = bf16[4,2,512,128]{3,2,1,0:T(8,128)(2,1)S(1)} collective-permute-done((bf16[4,2,512,128]{3,2,1,0:T(8,128)(2,1)}, bf16[4,2,512,128]{3,2,1,0:T(8,128)(2,1)S(1)}, u32[]{:S(2)}, u32[]{:S(2)}) %collective-permute-start.19) | collective-permute-done | bytes 1048608 | tf_op jit(solution)/shard_map/ppermute | solution.py:314
  343.7 28.1 %reduce-scatter.11.cloned.1.call-done = bf16[1,2,512,128]{3,2,1,0:T(8,128)(2,1)} async-done(((bf16[4,2,512,128]{3,2,1,0:T(8,128)(2,1)}), bf16[1,2,512,128]{3,2,1,0:T(8,128)(2,1)}) %reduce-scatter.11.cloned.1.call-update) | async-done | bytes 262160 | tf_op jit(solution)/shard_map/reduce_scatter | solution.py:323
  (118 shorter events, 60.9 us)
Async XLA Ops:
  7.2 113.0 %all-gather.2.cloned.1.call-start = ((), (), s32[]{:S(2)}) async-start(), calls=%async_computation.4 | async-start | bytes 9437184 | tf_op jit(solution)/shard_map/all_gather | solution.py:256
  7.2 15.2 %collective-permute-start = (bf16[512,512]{1,0:T(8,128)(2,1)}, bf16[512,512]{1,0:T(8,128)(2,1)S(1)}, u32[]{:S(2)}, u32[]{:S(2)}) collective-permute-start(bf16[512,512]{1,0:T(8,128)(2,1)} %param.7), channel_id=1, source_target_pairs={{0,16},{8,24},{16,0},{24,8},{1,17},{9,25},{17,1},{25,9},{2,18},{10... | collective-permute-start | bytes 1572872 | tf_op jit(solution)/shard_map/ppermute | solution.py:254
  23.5 264.0 %reduce-scatter.5.cloned.1.call-start = ((), (), s32[]{:S(2)}) async-start(), calls=%async_computation.5 | async-start | bytes 1310720 | tf_op jit(solution)/shard_map/reduce_scatter | solution.py:323
  23.5 43.3 %collective-permute-start.1 = (bf16[1024,896]{1,0:T(8,128)(2,1)}, bf16[1024,896]{1,0:T(8,128)(2,1)}, u32[]{:S(2)}, u32[]{:S(2)}) collective-permute-start(bf16[1024,896]{1,0:T(8,128)(2,1)} %get-tuple-element.93.refs_1_), channel_id=1, source_target_pairs={{0,8},{8,0},{16,24},{24,16},{1,9},{9,1},{17,25},{25,17},{2,10},{10... | collective-permute-start | bytes 5505032 | tf_op jit(solution)/shard_map/ppermute | solution.py:233
  25.3 79.1 %collective-permute-start.4 = (bf16[1024,896]{1,0:T(8,128)(2,1)S(1)}, bf16[1024,896]{1,0:T(8,128)(2,1)}, u32[]{:S(2)}, u32[]{:S(2)}) collective-permute-start(bf16[1024,896]{1,0:T(8,128)(2,1)S(1)} %get-tuple-element.91.refs_1_), channel_id=1, source_target_pairs={{0,8},{8,0},{16,24},{24,16},{1,9},{9,1},{17,25},{25,17},{2,10},{10... | collective-permute-start | bytes 5505032 | tf_op jit(solution)/shard_map/ppermute | solution.py:233
  25.6 43.3 %collective-permute-start.2 = (bf16[1024,896]{1,0:T(8,128)(2,1)}, bf16[1024,896]{1,0:T(8,128)(2,1)}, u32[]{:S(2)}, u32[]{:S(2)}) collective-permute-start(bf16[1024,896]{1,0:T(8,128)(2,1)} %get-tuple-element.92), channel_id=1, source_target_pairs={{0,16},{8,24},{16,0},{24,8},{1,17},{9,25},{17,1},{25,9},{2,18},{10... | collective-permute-start | bytes 5505032 | tf_op jit(solution)/shard_map/ppermute | solution.py:229
  27.4 78.5 %collective-permute-start.5 = (bf16[1024,896]{1,0:T(8,128)(2,1)}, bf16[1024,896]{1,0:T(8,128)(2,1)}, u32[]{:S(2)}, u32[]{:S(2)}) collective-permute-start(bf16[1024,896]{1,0:T(8,128)(2,1)} %get-tuple-element.90), channel_id=1, source_target_pairs={{0,16},{8,24},{16,0},{24,8},{1,17},{9,25},{17,1},{25,9},{2,18},{10... | collective-permute-start | bytes 5505032 | tf_op jit(solution)/shard_map/ppermute | solution.py:229
  29.9 76.0 %collective-permute-start.7 = (bf16[1792,512]{1,0:T(8,128)(2,1)S(1)}, bf16[1792,512]{1,0:T(8,128)(2,1)S(1)}, u32[]{:S(2)}, u32[]{:S(2)}) collective-permute-start(bf16[1792,512]{1,0:T(8,128)(2,1)S(1)} %get-tuple-element.88), channel_id=1, source_target_pairs={{0,1},{1,0},{2,3},{3,2},{4,5},{5,4},{6,7},{7,6},{8,9},{9,8},{10,11... | collective-permute-start | bytes 5505032 | tf_op jit(solution)/shard_map/ppermute | solution.py:242
  108.4 40.7 %collective-permute-start.8 = (bf16[1792,512]{1,0:T(8,128)(2,1)}, bf16[1792,512]{1,0:T(8,128)(2,1)}, u32[]{:S(2)}, u32[]{:S(2)}) collective-permute-start(bf16[1792,512]{1,0:T(8,128)(2,1)} %pad_maximum_fusion.1), channel_id=1, source_target_pairs={{0,16},{8,24},{16,0},{24,8},{1,17},{9,25},{17,1},{25,9},{2,18},{10... | collective-permute-start | bytes 5505032 | tf_op jit(solution)/shard_map/ppermute | solution.py:253
  110.4 44.7 %collective-permute-start.6 = (bf16[1024,896]{1,0:T(8,128)(2,1)}, bf16[1024,896]{1,0:T(8,128)(2,1)}, u32[]{:S(2)}, u32[]{:S(2)}) collective-permute-start(bf16[1024,896]{1,0:T(8,128)(2,1)} %collective-permute-done.5.refs_2_), channel_id=1, source_target_pairs={{0,8},{8,0},{16,24},{24,16},{1,9},{9,1},{17,25},{25,17},{2,10},{10... | collective-permute-start | bytes 5505032 | tf_op jit(solution)/shard_map/ppermute | solution.py:233
  118.1 93.3 %collective-permute-start.12 = (bf16[896,2048]{1,0:T(8,128)(2,1)}, bf16[896,2048]{1,0:T(8,128)(2,1)}, u32[]{:S(2)}, u32[]{:S(2)}) collective-permute-start(bf16[896,2048]{1,0:T(8,128)(2,1)} %shard_map.90), channel_id=1, source_target_pairs={{0,1},{1,0},{2,3},{3,2},{4,5},{5,4},{6,7},{7,6},{8,9},{9,8},{10,11... | collective-permute-start | bytes 11010056 | tf_op jit(solution)/shard_map/ppermute | solution.py:265
  118.2 74.8 %collective-permute-start.3 = (bf16[1024,896]{1,0:T(8,128)(2,1)}, bf16[1024,896]{1,0:T(8,128)(2,1)}, u32[]{:S(2)}, u32[]{:S(2)}) collective-permute-start(bf16[1024,896]{1,0:T(8,128)(2,1)} %collective-permute-done.2.refs_2_), channel_id=1, source_target_pairs={{0,8},{8,0},{16,24},{24,16},{1,9},{9,1},{17,25},{25,17},{2,10},{10... | collective-permute-start | bytes 5505032 | tf_op jit(solution)/shard_map/ppermute | solution.py:233
  153.0 55.7 %collective-permute-start.9 = (bf16[1792,256]{1,0:T(8,128)(2,1)S(1)}, bf16[1792,256]{1,0:T(8,128)(2,1)S(1)}, u32[]{:S(2)}, u32[]{:S(2)}) collective-permute-start(bf16[1792,256]{1,0:T(8,128)(2,1)S(1)} %pad_maximum_fusion.4.refs_8_), channel_id=1, source_target_pairs={{0,8},{8,0},{16,24},{24,16},{1,9},{9,1},{17,25},{25,17},{2,10},{10... | collective-permute-start | bytes 2752520 | tf_op jit(solution)/shard_map/ppermute | solution.py:233
  208.8 6.7 %collective-permute-start.11 = (bf16[1024,896]{1,0:T(8,128)(2,1)}, bf16[1024,896]{1,0:T(8,128)(2,1)}, u32[]{:S(2)}, u32[]{:S(2)}) collective-permute-start(bf16[1024,896]{1,0:T(8,128)(2,1)} %get-tuple-element.60.refs_2_), channel_id=1, source_target_pairs={{0,1},{1,0},{2,3},{3,2},{4,5},{5,4},{6,7},{7,6},{8,9},{9,8},{10,11... | collective-permute-start | bytes 5505032 | tf_op jit(solution)/shard_map/ppermute | solution.py:295
  209.3 22.6 %collective-permute-start.13 = (bf16[1792,256]{1,0:T(8,128)(2,1)}, bf16[1792,256]{1,0:T(8,128)(2,1)}, u32[]{:S(2)}, u32[]{:S(2)}) collective-permute-start(bf16[1792,256]{1,0:T(8,128)(2,1)} %pad_maximum_fusion.5.refs_9_), channel_id=1, source_target_pairs={{0,8},{8,0},{16,24},{24,16},{1,9},{9,1},{17,25},{25,17},{2,10},{10... | collective-permute-start | bytes 2752520 | tf_op jit(solution)/shard_map/ppermute | solution.py:233
  231.8 24.4 %collective-permute-start.14 = (bf16[4,2,512,128]{3,2,1,0:T(8,128)(2,1)}, bf16[4,2,512,128]{3,2,1,0:T(8,128)(2,1)S(1)}, u32[]{:S(2)}, u32[]{:S(2)}) collective-permute-start(bf16[4,2,512,128]{3,2,1,0:T(8,128)(2,1)} %get-tuple-element.65.refs_16_), channel_id=1, source_target_pairs={{0,16},{8,24},{16,0},{24,8},{1,17},{9,25},{17,1},{25,9},{2,18},{10... | collective-permute-start | bytes 3145736 | tf_op jit(solution)/shard_map/ppermute | solution.py:314
  232.8 21.3 %collective-permute-start.15 = (bf16[1792,256]{1,0:T(8,128)(2,1)}, bf16[1792,256]{1,0:T(8,128)(2,1)S(1)}, u32[]{:S(2)}, u32[]{:S(2)}) collective-permute-start(bf16[1792,256]{1,0:T(8,128)(2,1)} %pad_maximum_fusion.6.refs_10_), channel_id=1, source_target_pairs={{0,8},{8,0},{16,24},{24,16},{1,9},{9,1},{17,25},{25,17},{2,10},{10... | collective-permute-start | bytes 2752520 | tf_op jit(solution)/shard_map/ppermute | solution.py:233
  259.9 55.8 %reduce-scatter.7.cloned.1.call-start = ((), (), s32[]{:S(2)}) async-start(), calls=%async_computation.6 | async-start | bytes 1310720 | tf_op jit(solution)/shard_map/reduce_scatter | solution.py:323
  259.9 23.5 %collective-permute-start.16 = (bf16[4,2,512,128]{3,2,1,0:T(8,128)(2,1)S(1)}, bf16[4,2,512,128]{3,2,1,0:T(8,128)(2,1)}, u32[]{:S(2)}, u32[]{:S(2)}) collective-permute-start(bf16[4,2,512,128]{3,2,1,0:T(8,128)(2,1)S(1)} %copy-done.19), channel_id=1, source_target_pairs={{0,16},{8,24},{16,0},{24,8},{1,17},{9,25},{17,1},{25,9},{2,18},{10... | collective-permute-start | bytes 3145736 | tf_op jit(solution)/shard_map/ppermute | solution.py:314
  260.9 20.2 %collective-permute-start.17 = (bf16[1792,256]{1,0:T(8,128)(2,1)S(1)}, bf16[1792,256]{1,0:T(8,128)(2,1)S(1)}, u32[]{:S(2)}, u32[]{:S(2)}) collective-permute-start(bf16[1792,256]{1,0:T(8,128)(2,1)S(1)} %copy-done.7), channel_id=1, source_target_pairs={{0,8},{8,0},{16,24},{24,16},{1,9},{9,1},{17,25},{25,17},{2,10},{10... | collective-permute-start | bytes 2752520 | tf_op jit(solution)/shard_map/ppermute | solution.py:233
  287.5 56.2 %reduce-scatter.9.cloned.1.call-start = ((), (), s32[]{:S(2)}) async-start(), calls=%async_computation.7 | async-start | bytes 1310720 | tf_op jit(solution)/shard_map/reduce_scatter | solution.py:323
  287.5 24.8 %collective-permute-start.18 = (bf16[4,2,512,128]{3,2,1,0:T(8,128)(2,1)S(1)}, bf16[4,2,512,128]{3,2,1,0:T(8,128)(2,1)S(1)}, u32[]{:S(2)}, u32[]{:S(2)}) collective-permute-start(bf16[4,2,512,128]{3,2,1,0:T(8,128)(2,1)S(1)} %copy-done.18), channel_id=1, source_target_pairs={{0,16},{8,24},{16,0},{24,8},{1,17},{9,25},{17,1},{25,9},{2,18},{10... | collective-permute-start | bytes 3145736 | tf_op jit(solution)/shard_map/ppermute | solution.py:314
  315.7 56.0 %reduce-scatter.11.cloned.1.call-start = ((), (), s32[]{:S(2)}) async-start(), calls=%async_computation.8 | async-start | bytes 1310720 | tf_op jit(solution)/shard_map/reduce_scatter | solution.py:323
  315.8 25.0 %collective-permute-start.19 = (bf16[4,2,512,128]{3,2,1,0:T(8,128)(2,1)}, bf16[4,2,512,128]{3,2,1,0:T(8,128)(2,1)S(1)}, u32[]{:S(2)}, u32[]{:S(2)}) collective-permute-start(bf16[4,2,512,128]{3,2,1,0:T(8,128)(2,1)} %get-tuple-element.80), channel_id=1, source_target_pairs={{0,16},{8,24},{16,0},{24,8},{1,17},{9,25},{17,1},{25,9},{2,18},{10... | collective-permute-start | bytes 3145736 | tf_op jit(solution)/shard_map/ppermute | solution.py:314
  (25 other events, 302.5 us)
Sparse Core Ops, SparseCore 0:
  23.6 83.5 all-gather.1
  260.0 27.4 reduce-scatter.4
  289.9 25.7 reduce-scatter.6
  317.8 25.7 reduce-scatter.8
  345.9 25.8 reduce-scatter.10
